TPU v7x, 256 devices: a whole 4x4x8 slice. The times are simulated.
256 devices in a mesh: dp: 64 (over z, x, core), tensor: 4 (over y).
Axes of the slice: x: 4, y: 4, z: 8, core: 2. Of those that a mesh axis runs over, the one named last changes fastest.
Arguments:
- layer_input: bfloat16 [49152, 3584], P(('dp', 'tensor')), may hold values from -1.5 to 1.5
- output_grad: bfloat16 [49152, 1024], P('dp', 'tensor'), may hold values from -6 to 6
- query_weight: bfloat16 [3584, 1024], P(None, 'tensor'), may hold values from -0.09375 to 0.09375
- error_buffer: bfloat16 [64, 3584, 1024], P('dp', None, 'tensor'), may hold values from -48 to 48
- right_prev: float32 [1024, 64], P('tensor'), may hold values from -6 to 6
Outputs:
- input_grad: bfloat16 [49152, 3584], P(('dp', 'tensor'))
- right_factor: float32 [1024, 64], P('tensor')
- error_next: bfloat16 [64, 3584, 1024], P('dp', None, 'tensor')
All inputs are finite; a program needn't handle non-finite values.
Results may differ from a plain program's by a relative error of at most 0.0007.
Values may be sent and summed in bfloat16 or wider, within the bound.
No kernel may reach another device: no remote copies, remote signals or barrier semaphores. Data moves between devices by JAX's collectives and lax.ppermute only.
A program may use at most 128 MiB of HBM per device.

v0:
```python
import jax
import jax.numpy as jnp
from jax import lax
from jax.sharding import PartitionSpec as P


def orthonormal_rows(left_rows, gram_matrix):
    lower_factor = jnp.linalg.cholesky(gram_matrix)
    return jax.scipy.linalg.solve_triangular(lower_factor, left_rows.T, lower=True).T


def shards(layer_input, output_grad, query_weight, error_buffer, right_prev):
    highest = lax.Precision.HIGHEST
    replicas = lax.axis_size("dp")
    grad_rows = output_grad
    weight_grad = lax.dot_general(
        lax.all_gather(layer_input, "tensor", axis=0, tiled=True),
        grad_rows,
        (((0,), (0,)), ((), ())),
        preferred_element_type=jnp.float32,
    )
    merged = weight_grad + error_buffer[0].astype(jnp.float32)
    local_left = jnp.dot(merged, right_prev, precision=highest)
    left_mean = lax.psum(local_left, "dp") / replicas
    gram_matrix = jnp.dot(left_mean.T, left_mean, precision=highest)
    left_basis = orthonormal_rows(left_mean, gram_matrix)
    local_right = lax.dot_general(merged, left_basis, (((0,), (0,)), ((), ())), precision=highest)
    right_factor = lax.psum(local_right, "dp") / replicas
    approx = lax.dot_general(left_basis, right_factor, (((1,), (1,)), ((), ())), precision=highest)
    error_next = (merged - approx).astype(jnp.bfloat16)[None]
    grad_rows = output_grad
    input_grad = lax.psum_scatter(
        lax.dot_general(
            grad_rows, query_weight, (((1,), (1,)), ((), ())), preferred_element_type=jnp.float32
        ),
        "tensor",
        scatter_dimension=0,
        tiled=True,
    )
    return (input_grad.astype(jnp.bfloat16), right_factor, error_next)


def solution(mesh):
    in_specs = (
        P(("dp", "tensor"), None),
        P("dp", "tensor"),
        P(None, "tensor"),
        P("dp", None, "tensor"),
        P("tensor", None),
    )
    out_specs = (P(("dp", "tensor"), None), P("tensor", None), P("dp", None, "tensor"))
    return jax.shard_map(shards, mesh=mesh, in_specs=in_specs, out_specs=out_specs, check_vma=False)
```

profile of v0, /device:TPU:1, one launch (start us, length us, event | category | flops | bytes accessed | tf_op | source)
XLA Modules:
  0.0 574.3 jit_solution(1473574067061590577)
XLA Ops:
  7.2 0.0 copy-start
  7.2 0.0 all-gather.2.cloned.1.call-start
  7.2 0.7 all-gather.2.cloned.1.call-update
  7.9 0.0 copy-start.4
  7.9 0.0 all-reduce.3.cloned.1.call-start
  8.0 67.4 %all-gather.2.cloned.1.call-done = bf16[768,3584]{1,0:T(8,128)(2,1)} async-done(((bf16[192,3584]{1,0:T(8,128)(2,1)}), bf16[768,3584]{1,0:T(8,128)(2,1)}) %all-gather.2.cloned.1.call-update) | async-done | bytes 5505040 | tf_op jit(solution)/shard_map/all_gather | solution.py:17
  75.4 5.0 convolution_add_fusion
  80.4 0.0 copy-start.1
  80.4 1.9 copy-done.1
  82.3 0.0 copy-done.4
  82.3 4.6 fusion.14
  86.9 0.0 all-reduce.3.cloned.1.call-update
  86.9 0.0 copy-start.2
  86.9 0.0 all-reduce.5.cloned.1.call-start
  87.0 184.5 %all-reduce.3.cloned.1.call-done = f32[3584,64]{0,1:T(8,128)} async-done(((f32[3584,64]{0,1:T(8,128)}), f32[3584,64]{0,1:T(8,128)}) %all-reduce.3.cloned.1.call-update) | async-done | bytes 917520 | tf_op jit(solution)/shard_map/psum | solution.py:24
  271.5 2.4 fusion.4
  273.9 0.1 copy.8
  274.0 5.8 %cholesky.16 = f32[64,64]{1,0:T(8,128)S(1)} custom-call(f32[64,64]{1,0:T(8,128)S(1)} %fusion.10), custom_call_target="Cholesky" | custom-call | tf_op jit(solution)/shard_map/jit(cholesky)/cholesky | solution.py:8
  279.9 0.6 compare_reduce_fusion
  280.5 0.7 fusion.8
  281.2 4.9 custom-call.7
  286.1 2.1 fusion.2
  288.2 4.9 fusion.15
  293.1 0.0 all-reduce.5.cloned.1.call-update
  293.1 0.2 reduce-scatter.2.cloned.1.call-start
  293.4 0.0 copy-done
  293.4 0.0 copy-done.2
  293.4 5.8 %fusion.13 = f32[768,3584]{1,0:T(8,128)} fusion(bf16[768,256]{1,0:T(8,128)(2,1)S(1)} %copy-done.2, bf16[3584,256]{1,0:T(8,128)(2,1)S(1)} %copy-done), kind=kOutput, calls=%fused_computation.22 | convolution fusion | flops 1409286144 | bytes 13238272 | tf_op jit(solution)/shard_map/dot_general | solution.py:33
  299.2 0.0 reduce-scatter.2.cloned.1.call-update
  299.2 161.6 %all-reduce.5.cloned.1.call-done = f32[256,64]{0,1:T(8,128)} async-done(((f32[256,64]{0,1:T(8,128)}), f32[256,64]{0,1:T(8,128)}) %all-reduce.5.cloned.1.call-update) | async-done | bytes 65552 | tf_op jit(solution)/shard_map/psum | solution.py:28
  460.8 0.8 broadcast_multiply_fusion
  461.6 0.0 copy-start.3
  461.6 5.7 %fusion.1 = bf16[1,3584,256]{2,1,0:T(8,128)(2,1)} fusion(f32[3584,256]{1,0:T(8,128)} %copy-done.1, f32[64,3584]{1,0:T(8,128)S(1)} %fusion.2, f32[256,64]{0,1:T(8,128)S(1)} %broadcast_multiply_fusion), kind=kOutput, calls=%fused_computation.3 | convolution fusion | flops 706478080 | bytes 6488064 | tf_op jit(solution)/shard_map/dot_general | solution.py:29
  467.4 97.4 %reduce-scatter.2.cloned.1.call-done = f32[192,3584]{1,0:T(8,128)} async-done(((f32[768,3584]{1,0:T(8,128)}), f32[192,3584]{1,0:T(8,128)}) %reduce-scatter.2.cloned.1.call-update) | async-done | bytes 2752528 | tf_op jit(solution)/shard_map/reduce_scatter | solution.py:32
  564.7 3.0 convert_element_type.12
  567.7 0.0 copy-done.3
  (2 shorter events, 0.0 us)
Async XLA Ops:
  7.2 286.2 %copy-start = (bf16[3584,256]{1,0:T(8,128)(2,1)S(1)}, bf16[3584,256]{1,0:T(8,128)(2,1)}, u32[]{:S(2)}) copy-start(bf16[3584,256]{1,0:T(8,128)(2,1)} %param.7) | copy-start | bytes 5505028
  7.2 68.2 %all-gather.2.cloned.1.call-start = ((), (), s32[]{:S(2)}) async-start(), calls=%async_computation.2 | async-start | bytes 6881280 | tf_op jit(solution)/shard_map/all_gather | solution.py:17
  7.9 74.4 %copy-start.4 = (f32[256,64]{0,1:T(8,128)S(1)}, f32[256,64]{0,1:T(8,128)}, u32[]{:S(2)}) copy-start(f32[256,64]{0,1:T(8,128)} %param.9) | copy-start | bytes 196612
  7.9 263.6 %all-reduce.3.cloned.1.call-start = ((), (), s32[]{:S(2)}) async-start(), calls=%async_computation.3 | async-start | bytes 1835008 | tf_op jit(solution)/shard_map/psum | solution.py:24
  80.4 1.9 copy-start.1
  86.9 206.5 %copy-start.2 = (bf16[768,256]{1,0:T(8,128)(2,1)S(1)}, bf16[768,256]{1,0:T(8,128)(2,1)}, u32[]{:S(2)}) copy-start(bf16[768,256]{1,0:T(8,128)(2,1)} %param.6) | copy-start | bytes 1179652
  86.9 373.9 %all-reduce.5.cloned.1.call-start = ((), (), s32[]{:S(2)}) async-start(), calls=%async_computation.4 | async-start | bytes 131072 | tf_op jit(solution)/shard_map/psum | solution.py:28
  293.1 271.6 %reduce-scatter.2.cloned.1.call-start = ((), (), s32[]{:S(2)}) async-start(), calls=%async_computation.1 | async-start | bytes 13762560 | tf_op jit(solution)/shard_map/reduce_scatter | solution.py:32
  461.6 106.1 %copy-start.3 = (f32[256,64]{0,1:T(8,128)}, f32[256,64]{0,1:T(8,128)S(1)}, u32[]{:S(2)}) copy-start(f32[256,64]{0,1:T(8,128)S(1)} %broadcast_multiply_fusion) | copy-start | bytes 196612
Sparse Core Ops, SparseCore 0:
  9.8 65.4 all-gather.1
  87.0 184.4 all-reduce.2
  293.3 167.4 all-reduce.4
  463.4 101.2 reduce-scatter.1
where the time goes:
time: 575 us; the launch traced here: 574 us
  waiting for transfers between devices  512 us (89%)
  matrix products  30.6 us (5%)
  other arithmetic  15.9 us (3%)
  between operations  13.9 us (2%)
    psum x1, waiting for transfers between devices, shards(): left_mean = lax.psum(local_left, 'dp') / replicas  185 us
    psum x1, waiting for transfers between devices, shards(): right_factor = lax.psum(local_right, 'dp') / replicas  162 us
    reduce_scatter x1, waiting for transfers between devices, shards(): lax.psum_scatter(lax.dot_general(grad_rows, query_weight, (((1,), (1,)),...  97.4 us
    all_gather x1, waiting for transfers between devices, shards(): lax.all_gather(layer_input, 'tensor', axis=0, tiled=True)  67.4 us
  transfers between devices with their start and end apart: 4, of which 4 were waited for; matrix products, arithmetic and copies ran while one was open for 2% of the time, Pallas kernels for 0%

commit v1 on v0

v1 whole, which is shorter than its diff:
```python
import jax
import jax.numpy as jnp
from jax import lax
from jax.experimental import pallas as pl
from jax.experimental.pallas import tpu as pltpu
from jax.sharding import Mesh, PartitionSpec as P

F32, BF16 = jnp.float32, jnp.bfloat16
HIGHEST = lax.Precision.HIGHEST
FEATURES, COLUMNS, RANK, SEQ, PART = 3584, 256, 64, 768, 192
HALF = RANK // 2
REPLICAS = 64
STEP = 896
TILES = (8, 4, 7, 4, 128)
HALF_FEATURES, FIRST = FEATURES // 2, 1024
PLANE = ("z", "x")
SMALL = pl.CostEstimate(flops=1000, bytes_accessed=1000, transcendentals=0)
VMEM = pltpu.CompilerParams(vmem_limit_bytes=40 * 2**20)
ALL_VMEM = pltpu.CompilerParams(vmem_limit_bytes=60 * 2**20)


def dot(a, b, dim_a, dim_b, precision=None):
    return lax.dot_general(
        a, b, (((dim_a,), (dim_b,)), ((), ())), precision=precision, preferred_element_type=F32
    )


def whole(array):
    return pl.BlockSpec(array.shape, lambda i: (0,) * array.ndim)


def shift(value, axis, size, by):
    return lax.ppermute(value, axis, [(at, (at + by) % size) for at in range(size)])


def split(value):
    high = value.astype(BF16)
    rest = value - high.astype(F32)
    middle = rest.astype(BF16)
    return high, middle, (rest - middle.astype(F32)).astype(BF16)


def stacked_dot(a, b, dim_b):
    rows = a.shape[0]
    stack = jnp.concatenate(split(a), 0)
    high, middle, low = split(b)
    first = dot(stack, high, 1, dim_b)
    second = dot(stack[: 2 * rows], middle, 1, dim_b)
    third = dot(stack[:rows], low, 1, dim_b)
    small = first[2 * rows :] + second[rows:] + third
    return first[:rows] + (first[rows : 2 * rows] + second[:rows] + small)


def merged_and_left(core, pieces, grads, error, right, offset, before):
    chunk = pieces[0].shape[1]
    first = offset // STEP
    count = len(pieces)

    def body(core_ref, *refs):
        piece_refs = refs[:count]
        grad_ref, error_ref, right_ref = refs[count : count + 3]
        merged_ref, mine_ref, other_ref = refs[-3:]
        tokens = jnp.concatenate([ref[...] for ref in piece_refs], 0)
        transposed = dot(grad_ref[...], tokens, 0, 0)
        merged = transposed.T + error_ref[...].astype(F32)
        merged_ref[...] = merged
        left = stacked_dot(right_ref[...], merged, 1)
        low, high = left[:HALF], left[HALF:]
        is_first = core_ref[0] == 0
        mine, other = jnp.where(is_first, low, high), jnp.where(is_first, high, low)
        for row in range(8):
            for lane in range(7):
                tile = slice(row * 4, row * 4 + 4), slice(lane * 128, lane * 128 + 128)
                mine_ref[row, 0, lane] = mine[tile]
                other_ref[row, 0, lane] = other[tile]

    aliased = [] if before is None else list(before)
    tiles = pl.BlockSpec((8, 1, 7, 4, 128), lambda i: (0, first + i, 0, 0, 0))
    return pl.pallas_call(
        body,
        grid=(chunk // STEP,),
        in_specs=[pl.BlockSpec(memory_space=pltpu.SMEM)]
        + [pl.BlockSpec((piece.shape[0], STEP), lambda i: (0, i)) for piece in pieces]
        + [whole(grads), pl.BlockSpec((STEP, COLUMNS), lambda i: (first + i, 0)), whole(right)]
        + [pl.BlockSpec(memory_space=pl.ANY) for _ in aliased],
        out_specs=[pl.BlockSpec((STEP, COLUMNS), lambda i: (first + i, 0)), tiles, tiles],
        out_shape=[
            jax.ShapeDtypeStruct((FEATURES, COLUMNS), F32),
            jax.ShapeDtypeStruct(TILES, F32),
            jax.ShapeDtypeStruct(TILES, F32),
        ],
        input_output_aliases={4 + count + at: at for at in range(len(aliased))},
        compiler_params=ALL_VMEM,
        cost_estimate=SMALL,
        name="merged_and_left",
    )(core, *pieces, grads, error, right, *aliased)


def ordered(core, mine, other):
    first = core == 0
    return jnp.concatenate([jnp.where(first, mine, other), jnp.where(first, other, mine)], 0)


def products(core, mine, other, merged):
    def body(core_ref, mine_ref, other_ref, merged_ref, left_ref, cross_ref, gram_ref):
        @pl.when(pl.program_id(0) == 0)
        def _():
            cross_ref[...] = jnp.zeros_like(cross_ref)
            gram_ref[...] = jnp.zeros_like(gram_ref)

        def rows(ref):
            return jnp.concatenate(
                [jnp.concatenate([ref[row, 0, lane] for lane in range(7)], 1) for row in range(8)],
                0,
            )

        left = ordered(core_ref[0], rows(mine_ref), rows(other_ref))
        left_ref[...] = left
        stack = jnp.concatenate(split(left), 0)
        squares = dot(stack, stack, 1, 1)

        def square(a, b):
            return squares[a * RANK : (a + 1) * RANK, b * RANK : (b + 1) * RANK]

        small = square(0, 2) + square(2, 0) + square(1, 1)
        gram_ref[...] += square(0, 0) + (square(0, 1) + square(1, 0) + small)
        cross_ref[...] += stacked_dot(left, merged_ref[...], 0)

    tiles = pl.BlockSpec((8, 1, 7, 4, 128), lambda i: (0, i, 0, 0, 0))
    return pl.pallas_call(
        body,
        grid=(FEATURES // STEP,),
        in_specs=[
            pl.BlockSpec(memory_space=pltpu.SMEM),
            tiles,
            tiles,
            pl.BlockSpec((STEP, COLUMNS), lambda i: (i, 0)),
        ],
        out_specs=[
            pl.BlockSpec((RANK, STEP), lambda i: (0, i)),
            pl.BlockSpec((RANK, COLUMNS), lambda i: (0, 0)),
            pl.BlockSpec((RANK, RANK), lambda i: (0, 0)),
        ],
        out_shape=[
            jax.ShapeDtypeStruct((RANK, FEATURES), F32),
            jax.ShapeDtypeStruct((RANK, COLUMNS), F32),
            jax.ShapeDtypeStruct((RANK, RANK), F32),
        ],
        compiler_params=VMEM,
        cost_estimate=SMALL,
        name="cross_and_gram",
    )(core, mine, other, merged)


def inverse_factor(gram):
    def body(gram_ref, inverse_ref):
        rows = lax.broadcasted_iota(jnp.int32, (RANK, 2 * RANK), 0)
        lanes = lax.broadcasted_iota(jnp.int32, (RANK, 2 * RANK), 1)
        work = jnp.concatenate([gram_ref[...], jnp.zeros((RANK, RANK), F32)], 1)
        work = jnp.where(lanes == rows + RANK, 1.0, work)
        for at in range(RANK):
            pivot_row = work[at : at + 1, :]
            factor = work[:, at : at + 1] * (1.0 / pivot_row[:, at : at + 1])
            work = jnp.where(rows > at, work - factor * pivot_row, work)
        pivots = jnp.sum(jnp.where(lanes == rows, work, 0.0), 1, keepdims=True)
        inverse_ref[...] = work[:, RANK:] * (1.0 / jnp.sqrt(pivots))

    return pl.pallas_call(
        body,
        out_shape=jax.ShapeDtypeStruct((RANK, RANK), F32),
        cost_estimate=SMALL,
        name="inverse_factor",
    )(gram)


def orthonormal(inverse, left, block):
    def body(inverse_ref, left_ref, basis_ref):
        basis = stacked_dot(inverse_ref[...], left_ref[...], 0).T
        high = basis.astype(BF16)
        low = (basis - high.astype(F32)).astype(BF16)
        basis_ref[...] = jnp.concatenate([high, low], 1)

    return pl.pallas_call(
        body,
        grid=(FEATURES // block,),
        in_specs=[whole(inverse), pl.BlockSpec((RANK, block), lambda i: (0, i))],
        out_specs=pl.BlockSpec((block, 2 * RANK), lambda i: (i, 0)),
        out_shape=jax.ShapeDtypeStruct((FEATURES, 2 * RANK), BF16),
        compiler_params=VMEM,
        cost_estimate=SMALL,
        name="orthonormal",
    )(inverse, left)


def finish(core, mine, other, inverse, basis, merged, block):
    def body(core_ref, mine_ref, other_ref, inverse_ref, basis_ref, merged_ref, *refs):
        error_ref, right_ref, parts_ref = refs

        @pl.when(pl.program_id(0) == 0)
        def _():
            cross = ordered(core_ref[0], mine_ref[...], other_ref[...])
            right = dot(inverse_ref[...], cross, 1, 0, HIGHEST)
            right_ref[...] = right
            high = right.astype(BF16)
            low = (right - high.astype(F32)).astype(BF16)
            parts_ref[...] = jnp.concatenate([high, high, low, low], 0)

        both = jnp.concatenate([basis_ref[...], basis_ref[...]], 1)
        approx = dot(both, parts_ref[...], 1, 0)
        error_ref[...] = (merged_ref[...] - approx).astype(BF16)

    rows = pl.BlockSpec((block, COLUMNS), lambda i: (i, 0))
    return pl.pallas_call(
        body,
        grid=(FEATURES // block,),
        in_specs=[
            pl.BlockSpec(memory_space=pltpu.SMEM),
            whole(mine),
            whole(other),
            whole(inverse),
            pl.BlockSpec((block, 2 * RANK), lambda i: (i, 0)),
            rows,
        ],
        out_specs=[rows, pl.BlockSpec((RANK, COLUMNS), lambda i: (0, 0))],
        out_shape=[
            jax.ShapeDtypeStruct((FEATURES, COLUMNS), BF16),
            jax.ShapeDtypeStruct((RANK, COLUMNS), F32),
        ],
        scratch_shapes=[pltpu.VMEM((4 * RANK, COLUMNS), BF16)],
        compiler_params=VMEM,
        cost_estimate=SMALL,
        name="finish",
    )(core, mine, other, inverse, basis, merged)


def input_gradient(core, grads, weight, mine, other):
    def body(core_ref, grad_ref, weight_ref, *refs):
        *parcel_refs, out_ref = refs
        before_high, far, after_high = parcel_refs[1], parcel_refs[4], parcel_refs[3]
        blocks = [
            grad_ref[...],
            before_high[HALF_FEATURES - FIRST :, :],
            far[HALF_FEATURES:, :],
            after_high[HALF_FEATURES - FIRST :, :],
        ]
        for side in range(2):
            half = core_ref[0] if side == 0 else 1 - core_ref[0]
            before_low, before_high, after_low, after_high, far = parcel_refs[
                5 * side : 5 * side + 5
            ]
            for first, count, near in (
                (0, FIRST, (before_low, after_low)),
                (FIRST, HALF_FEATURES - FIRST, (before_high, after_high)),
            ):
                start = pl.multiple_of(half * HALF_FEATURES + first, 128)
                total = dot(blocks[0], weight_ref[pl.ds(start, count), :], 1, 1)
                total = total + dot(blocks[1], near[0][:count, :], 1, 1)
                total = total + dot(blocks[2], far[first : first + count, :], 1, 1)
                total = total + dot(blocks[3], near[1][:count, :], 1, 1)
                out_ref[:, pl.ds(start, count)] = total.astype(BF16)

    vmem = pl.BlockSpec(memory_space=pltpu.VMEM)
    return pl.pallas_call(
        body,
        in_specs=[pl.BlockSpec(memory_space=pltpu.SMEM)] + [vmem] * 12,
        out_specs=vmem,
        out_shape=jax.ShapeDtypeStruct((PART, FEATURES), BF16),
        compiler_params=VMEM,
        cost_estimate=SMALL,
        name="input_gradient",
    )(core, grads, weight, *mine, *other)


def both_ways(value):
    return shift(value, "tensor", 4, 1), shift(value, "tensor", 4, -1)


def shards(layer_input, output_grad, query_weight, error_buffer, right_prev):
    core = lax.axis_index("c")
    place = lax.axis_index("tensor")
    error = error_buffer[0]
    core_word = core.astype(jnp.int32).reshape(1)

    grads = lax.dynamic_slice_in_dim(
        jnp.concatenate([output_grad, output_grad], 0), place * PART, SEQ, 0
    )
    right_rows = right_prev.T

    cut = FEATURES // 2
    chunks = [layer_input[:, :cut], layer_input[:, cut:]]
    near = [both_ways(chunk) for chunk in chunks]
    far = [
        (shift(before[:96], "tensor", 4, 1), shift(after[96:], "tensor", 4, -1))
        for before, after in near
    ]
    state = None
    for at, chunk in enumerate(chunks):
        before, after = near[at]
        pieces = (chunk, after, *far[at], before)
        state = merged_and_left(core_word, pieces, grads, error, right_rows, at * cut, state)
    merged, mine, other = state

    half = lax.dynamic_slice_in_dim(query_weight, core * HALF_FEATURES, HALF_FEATURES, 0)
    low, high = half[:FIRST], half[FIRST:]
    before, far_parcel, after = (
        jnp.concatenate([rows, grads[k * PART : (k + 1) * PART]], 0)
        for rows, k in ((high, 1), (half, 2), (high, 3))
    )
    low, before, far_parcel, after = lax.optimization_barrier(
        (low, before, far_parcel, after, near[1][0])
    )[:4]
    lows = both_ways(low)

    total = (mine + shift(other, "c", 2, 1)).reshape(32, 7, 4, 128)
    blocks = lax.all_to_all(total, PLANE, 0, 0, tiled=True)
    reduced = jnp.sum(blocks, 0) * (1 / REPLICAS)
    reduced, *lows = lax.optimization_barrier((reduced, *lows))
    parcels = (
        lows[0],
        shift(before, "tensor", 4, 1),
        lows[1],
        shift(after, "tensor", 4, -1),
        shift(far_parcel, "tensor", 4, 2),
    )
    copies = jnp.broadcast_to(reduced, (32, 7, 4, 128))
    mine = lax.all_to_all(copies, PLANE, 0, 0, tiled=True).reshape(TILES)
    other = shift(mine, "c", 2, 1)

    left, cross, gram = products(core_word, mine, other, merged)
    inverse = inverse_factor(gram)

    mine = lax.dynamic_slice_in_dim(cross, core * HALF, HALF, 0)
    other = lax.dynamic_slice_in_dim(cross, (1 - core) * HALF, HALF, 0)
    mine = (mine + shift(other, "c", 2, 1)) * (1 / REPLICAS)
    copies = jnp.broadcast_to(mine[None], (4, HALF, COLUMNS))
    mine = jnp.sum(lax.all_to_all(copies, "x", 0, 0, tiled=True), 0)

    mine, inverse, *parcels = lax.optimization_barrier((mine, inverse, *parcels))
    other_parcels = [shift(parcel, "c", 2, 1) for parcel in parcels]
    basis = orthonormal(inverse, left, 896)
    input_grad = input_gradient(core_word, grads[:PART], query_weight, parcels, other_parcels)

    copies = jnp.broadcast_to(mine[None], (8, HALF, COLUMNS))
    blocks = lax.all_to_all(copies, "z", 0, 0, tiled=True)
    blocks, basis, input_grad = lax.optimization_barrier((blocks, basis, input_grad))
    mine = jnp.sum(blocks, 0)
    other = shift(mine, "c", 2, 1)

    error_next, right = finish(core_word, mine, other, inverse, basis, merged, 896)
    return input_grad, right.T, error_next[None]


def solution(mesh):
    split = Mesh(mesh.devices.reshape(8, 4, 2, 4), ("z", "x", "c", "tensor"))
    dp = ("z", "x", "c")
    in_specs = (
        P((*dp, "tensor"), None),
        P(dp, "tensor"),
        P(None, "tensor"),
        P(dp, None, "tensor"),
        P("tensor", None),
    )
    out_specs = (P((*dp, "tensor"), None), P("tensor", None), P(dp, None, "tensor"))
    return jax.shard_map(
        shards, mesh=split, in_specs=in_specs, out_specs=out_specs, check_vma=False
    )
```

time: 575 us -> 164 us (0.29)
  waiting for transfers between devices: 512 us -> 56.1 us
  starting transfers between devices: 0.34 us -> 55.3 us
  matrix products: 30.6 us -> 0 us
  Pallas kernels: 0 us -> 30.2 us
  between operations: 13.9 us -> 0.9 us
  local copies, waits for them, and re-layouts: 1.99 us -> 14.6 us
  other arithmetic: 15.9 us -> 5.82 us
    psum x2 -> x0, waiting for transfers between devices: 346 us -> none  [the longest x1 185 us: shards(): left_mean = lax.psum(local_left, 'dp') / replicas]
    reduce_scatter x1 -> x0, waiting for transfers between devices: 97.4 us -> none  [shards(): lax.psum_scatter(lax.dot_general(grad_rows, query_weight, (((1,), (1,)),...]
    all_gather x1 -> x0, waiting for transfers between devices: 67.4 us -> none  [shards(): lax.all_gather(layer_input, 'tensor', axis=0, tiled=True)]
    pallas_call x0 -> x7, Pallas kernels: none -> 30.2 us  [the longest x2 9.72 us: merged_and_left(): pl.pallas_call(body, grid=(chunk // STEP,), in_specs=[pl.BlockSpec(memory...]
    ppermute x0 -> x22, waiting for transfers between devices: none -> 29.3 us  [shift(): lax.ppermute(value, axis, [(at, (at + by) % size) for at in range(size)])]
    dot_general x6 -> x0, matrix products: 28.4 us -> none  [the longest x1 5.8 us: shards(): lax.dot_general(grad_rows, query_weight, (((1,), (1,)), ((), ())), prefer...]
    ppermute x0 -> x22, starting transfers between devices: none -> 27.8 us  [shift(): lax.ppermute(value, axis, [(at, (at + by) % size) for at in range(size)])]
    all_to_all x0 -> x4, starting transfers between devices: none -> 27.5 us  [the longest x1 10.7 us: shards(): blocks = lax.all_to_all(total, PLANE, 0, 0, tiled=True)]
  transfers between devices with their start and end apart: 4 -> 26, of which waited for: 4 -> 13; matrix products, arithmetic and copies ran while one was open for 2% -> 5% of each run, Pallas kernels for 0% -> 14%
where the time goes in v1:
time: 164 us; the launch traced here: 163 us
  waiting for transfers between devices  56.1 us (34%)
  starting transfers between devices  55.3 us (34%)
  Pallas kernels  30.2 us (18%)
  local copies, waits for them, and re-layouts  14.6 us (9%)
  other arithmetic  5.82 us (4%)
    ppermute x22, waiting for transfers between devices, shift(): lax.ppermute(value, axis, [(at, (at + by) % size) for at in range(size)])  29.3 us
    ppermute x22, starting transfers between devices, shift(): lax.ppermute(value, axis, [(at, (at + by) % size) for at in range(size)])  27.8 us
    all_to_all x1, waiting for transfers between devices, shards(): mine = lax.all_to_all(copies, PLANE, 0, 0, tiled=True).reshape(TILES)  13.3 us
    all_to_all x1, waiting for transfers between devices, shards(): blocks = lax.all_to_all(total, PLANE, 0, 0, tiled=True)  11.6 us
    all_to_all x1, starting transfers between devices, shards(): blocks = lax.all_to_all(total, PLANE, 0, 0, tiled=True)  10.7 us
    pallas_call x2, Pallas kernels, merged_and_left(): pl.pallas_call(body, grid=(chunk // STEP,), in_specs=[pl.BlockSpec(memory...  9.72 us
    all_to_all x1, starting transfers between devices, shards(): mine = lax.all_to_all(copies, PLANE, 0, 0, tiled=True).reshape(TILES)  8.92 us
    unnamed x34, local copies, waits for them, and re-layouts  7.59 us
  transfers between devices with their start and end apart: 26, of which 13 were waited for; matrix products, arithmetic and copies ran while one was open for 5% of the time, Pallas kernels for 14%

profile of v1, /device:TPU:1, one launch (start us, length us, event | category | flops | bytes accessed | tf_op | source)
XLA Modules:
  0.0 162.8 jit_solution(6030141259427961176)
XLA Ops:
  0.6 1.4 fusion.1
  2.1 2.2 %collective-permute-start.5 = (bf16[192,1792]{1,0:T(8,128)(2,1)S(1)}, bf16[192,1792]{1,0:T(8,128)(2,1)S(1)}, u32[]{:S(2)}, u32[]{:S(2)}) collective-permute-start(bf16[192,1792]{1,0:T(8,128)(2,1)S(1)} %get-tuple-element.59.refs_0_), channel_id=1, source_target_pairs={{0,1},{1,2},{2,3},{3,0},{4,5},{5,6},{6,7},{7,4},{8,9},{9,10},{10,1... | collective-permute-start | bytes 2064392 | tf_op jit(solution)/shard_map/ppermute | solution.py:33
  4.3 1.5 collective-permute-start.4
  5.8 2.7 %collective-permute-start = (bf16[192,1792]{1,0:T(8,128)(2,1)S(1)}, bf16[192,1792]{1,0:T(8,128)(2,1)S(1)}, u32[]{:S(2)}, u32[]{:S(2)}) collective-permute-start(bf16[192,1792]{1,0:T(8,128)(2,1)S(1)} %get-tuple-element.60.refs_0_), channel_id=1, source_target_pairs={{0,3},{1,0},{2,1},{3,2},{4,7},{5,4},{6,5},{7,6},{8,11},{9,8},{10,9... | collective-permute-start | bytes 2064392 | tf_op jit(solution)/shard_map/ppermute | solution.py:33
  8.5 10.4 %collective-permute-done.5.refs_4_ = bf16[192,1792]{1,0:T(8,128)(2,1)S(1)} collective-permute-done((bf16[192,1792]{1,0:T(8,128)(2,1)S(1)}, bf16[192,1792]{1,0:T(8,128)(2,1)S(1)}, u32[]{:S(2)}, u32[]{:S(2)}) %collective-permute-start.5) | collective-permute-done | bytes 688160 | tf_op jit(solution)/shard_map/ppermute | solution.py:33
  18.8 0.8 slice.50
  19.6 1.6 collective-permute-start.6
  21.2 0.8 slice.51
  22.0 1.6 %collective-permute-start.7 = (bf16[96,1792]{1,0:T(8,128)(2,1)}, bf16[96,1792]{1,0:T(8,128)(2,1)}, u32[]{:S(2)}, u32[]{:S(2)}) collective-permute-start(bf16[96,1792]{1,0:T(8,128)(2,1)} %slice.51), channel_id=1, source_target_pairs={{0,3},{1,0},{2,1},{3,2},{4,7},{5,4},{6,5},{7,6},{8,11},{9,8},{10,9... | collective-permute-start | bytes 1032200 | tf_op jit(solution)/shard_map/ppermute | solution.py:33
  23.6 9.9 %collective-permute-done.1.refs_4_ = bf16[192,1792]{1,0:T(8,128)(2,1)S(1)} collective-permute-done((bf16[192,1792]{1,0:T(8,128)(2,1)S(1)}, bf16[192,1792]{1,0:T(8,128)(2,1)S(1)}, u32[]{:S(2)}, u32[]{:S(2)}) %collective-permute-start.1) | collective-permute-done | bytes 688160 | tf_op jit(solution)/shard_map/ppermute | solution.py:33
  33.6 0.8 slice.48
  34.4 1.6 collective-permute-start.2
  35.9 0.8 slice.49
  36.7 1.6 %collective-permute-start.3 = (bf16[96,1792]{1,0:T(8,128)(2,1)}, bf16[96,1792]{1,0:T(8,128)(2,1)}, u32[]{:S(2)}, u32[]{:S(2)}) collective-permute-start(bf16[96,1792]{1,0:T(8,128)(2,1)} %slice.49), channel_id=1, source_target_pairs={{0,3},{1,0},{2,1},{3,2},{4,7},{5,4},{6,5},{7,6},{8,11},{9,8},{10,9... | collective-permute-start | bytes 1032200 | tf_op jit(solution)/shard_map/ppermute | solution.py:33
  38.4 1.8 %fusion.refs_5_ = bf16[768,256]{1,0:T(8,128)(2,1)} fusion(s32[]{:T(128)S(6)} %select_n.12, bf16[768,256]{1,0:T(8,128)(2,1)S(1)} %copy-done.16), kind=kLoop, calls=%fused_computation.5 | loop fusion | flops 786432 | bytes 786436 | tf_op jit(solution)/shard_map/concatenate | solution.py:285
  40.2 0.9 collective-permute-done.6.refs_2_
  41.1 1.2 collective-permute-done.7.refs_3_
  42.2 4.8 %merged_and_left.2 = (f32[3584,256]{1,0:T(8,128)}, f32[8,4,7,4,128]{4,3,2,1,0:T(4,128)}, f32[8,4,7,4,128]{4,3,2,1,0:T(4,128)}) custom-call(s32[1]{0:T(128)} %bitcast.core_ref, bf16[192,1792]{1,0:T(8,128)(2,1)} %copy-done.10, bf16[192,1792]{1,0:T(8,128)(2,1)} %copy-done.15, bf16[96,1792]{1,0:T(8,128)(2,1)} %collective-permute-done.6.refs_2_, ...), custom_call_target="tpu_custom_call" | custom-call | flops 1000 | bytes 1000 | tf_op jit(solution)/shard_map/merged_and_left/pallas_call | solution.py:79
  47.0 1.4 collective-permute-done.2.refs_2_
  48.4 1.2 collective-permute-done.3.refs_3_
  49.6 4.9 %merged_and_left.3 = (f32[3584,256]{1,0:T(8,128)}, f32[8,4,7,4,128]{4,3,2,1,0:T(4,128)}, f32[8,4,7,4,128]{4,3,2,1,0:T(4,128)}) custom-call(s32[1]{0:T(128)} %bitcast.core_ref, bf16[192,1792]{1,0:T(8,128)(2,1)} %copy-done.9, bf16[192,1792]{1,0:T(8,128)(2,1)} %copy-done.13, ...), custom_call_target="tpu_custom_call", output_to_operand_aliasing={{0}: (9, {}), {1}: (10, {}), {2}: (11, {})} | custom-call | flops 1000 | bytes 1000 | tf_op jit(solution)/shard_map/merged_and_left/pallas_call | solution.py:79
  54.5 2.6 %collective-permute-start.8 = (f32[8,4,7,4,128]{4,3,2,1,0:T(4,128)}, f32[8,4,7,4,128]{4,3,2,1,0:T(4,128)S(1)}, u32[]{:S(2)}, u32[]{:S(2)}) collective-permute-start(f32[8,4,7,4,128]{4,3,2,1,0:T(4,128)} %get-tuple-element.35), channel_id=1, source_target_pairs={{0,4},{4,0},{1,5},{5,1},{2,6},{6,2},{3,7},{7,3},{8,12},{12,8},{9,1... | collective-permute-start | bytes 1376264 | tf_op jit(solution)/shard_map/ppermute | solution.py:33
  57.2 1.0 pad_maximum_fusion.2
  58.2 0.5 collective-permute-done.8
  58.7 0.9 add.19
  59.6 10.7 %all-to-all-start = ((f32[32,7,4,128]{3,2,1,0:T(4,128)}), f32[32,7,4,128]{3,2,1,0:T(4,128)S(1)}, u32[]{:S(2)}, u32[]{:S(2)}) async-start(f32[32,7,4,128]{3,2,1,0:T(4,128)} %bitcast.3), calls=%async_computation | async-start | bytes 917504 | tf_op jit(solution)/shard_map/all_to_all | solution.py:315
  70.4 0.1 constant_dynamic-slice_fusion.2
  70.4 1.0 pad_maximum_fusion
  71.5 2.7 %collective-permute-start.10 = (bf16[1024,256]{1,0:T(8,128)(2,1)S(1)}, bf16[1024,256]{1,0:T(8,128)(2,1)S(1)}, u32[]{:S(2)}, u32[]{:S(2)}) collective-permute-start(bf16[1024,256]{1,0:T(8,128)(2,1)S(1)} %constant_dynamic-slice_fusion), channel_id=1, source_target_pairs={{0,3},{1,0},{2,1},{3,2},{4,7},{5,4},{6,5},{7,6},{8,11},{9,8},{10,9... | collective-permute-start | bytes 1572872 | tf_op jit(solution)/shard_map/ppermute | solution.py:33
  74.2 11.6 %all-to-all-done = f32[32,7,4,128]{3,2,1,0:T(4,128)S(1)} async-done(((f32[32,7,4,128]{3,2,1,0:T(4,128)}), f32[32,7,4,128]{3,2,1,0:T(4,128)S(1)}, u32[]{:S(2)}, u32[]{:S(2)}) %all-to-all-start) | async-done | bytes 458784 | tf_op jit(solution)/shard_map/all_to_all | solution.py:315
  85.8 0.1 reduce_sum.27
  85.9 2.1 %collective-permute-done.9.refs_0_ = bf16[1024,256]{1,0:T(8,128)(2,1)} collective-permute-done((bf16[1024,256]{1,0:T(8,128)(2,1)S(1)}, bf16[1024,256]{1,0:T(8,128)(2,1)}, u32[]{:S(2)}, u32[]{:S(2)}) %collective-permute-start.9) | collective-permute-done | bytes 524320 | tf_op jit(solution)/shard_map/ppermute | solution.py:33
  88.0 0.8 broadcast_in_dim.8
  88.8 8.9 %all-to-all-start.1 = ((f32[32,7,4,128]{3,2,1,0:T(4,128)}), f32[32,7,4,128]{3,2,1,0:T(4,128)S(1)}, u32[]{:S(2)}, u32[]{:S(2)}) async-start(f32[32,7,4,128]{3,2,1,0:T(4,128)} %broadcast_in_dim.8), calls=%async_computation.1 | async-start | bytes 917504 | tf_op jit(solution)/shard_map/all_to_all | solution.py:326
  97.8 0.1 collective-permute-start.15
  97.9 13.3 %all-to-all-done.1 = f32[32,7,4,128]{3,2,1,0:T(4,128)S(1)} async-done(((f32[32,7,4,128]{3,2,1,0:T(4,128)}), f32[32,7,4,128]{3,2,1,0:T(4,128)S(1)}, u32[]{:S(2)}, u32[]{:S(2)}) %all-to-all-start.1) | async-done | bytes 458784 | tf_op jit(solution)/shard_map/all_to_all | solution.py:326
  111.2 4.3 %collective-permute-start.11 = (f32[8,4,7,4,128]{4,3,2,1,0:T(4,128)S(1)}, f32[8,4,7,4,128]{4,3,2,1,0:T(4,128)S(1)}, u32[]{:S(2)}, u32[]{:S(2)}) collective-permute-start(f32[8,4,7,4,128]{4,3,2,1,0:T(4,128)S(1)} %bitcast.7), channel_id=1, source_target_pairs={{0,4},{4,0},{1,5},{5,1},{2,6},{6,2},{3,7},{7,3},{8,12},{12,8},{9,1... | collective-permute-start | bytes 1376264 | tf_op jit(solution)/shard_map/ppermute | solution.py:33
  115.5 2.7 %collective-permute-start.14 = (bf16[960,256]{1,0:T(8,128)(2,1)}, bf16[960,256]{1,0:T(8,128)(2,1)}, u32[]{:S(2)}, u32[]{:S(2)}) collective-permute-start(bf16[960,256]{1,0:T(8,128)(2,1)} %get-tuple-element.44), channel_id=1, source_target_pairs={{0,3},{1,0},{2,1},{3,2},{4,7},{5,4},{6,5},{7,6},{8,11},{9,8},{10,9... | collective-permute-start | bytes 1474568 | tf_op jit(solution)/shard_map/ppermute | solution.py:33
  118.2 2.0 %copy-done = f32[3584,256]{1,0:T(8,128)S(1)} copy-done((f32[3584,256]{1,0:T(8,128)S(1)}, f32[3584,256]{1,0:T(8,128)}, u32[]{:S(2)}) %copy-start) | copy-done | bytes 3670040
  120.2 2.5 %cross_and_gram.1 = (f32[64,3584]{1,0:T(8,128)S(1)}, f32[64,256]{1,0:T(8,128)S(1)}, f32[64,64]{1,0:T(8,128)S(1)}) custom-call(s32[1]{0:T(128)} %bitcast.core_ref, f32[8,4,7,4,128]{4,3,2,1,0:T(4,128)S(1)} %bitcast.8, f32[8,4,7,4,128]{4,3,2,1,0:T(4,128)S(1)} %collective-permute-done.11.other_ref, f32[3584,256]{1,0:T(8,128)S(1)} %copy-done), custom_call_target="tpu_custom_call" | custom-call | flops 1000 | bytes 1000 | tf_op jit(solution)/shard_map/cross_and_gram/pallas_call | solution.py:130
  122.8 0.9 copy-done.3
  123.7 0.6 copy-done.7
  124.3 0.6 collective-permute-start.12
  124.9 0.9 collective-permute-done.12
  125.8 0.7 broadcast_in_dim.9
  126.4 3.3 %all-to-all-start.2 = ((f32[4,32,256]{2,1,0:T(8,128)}), f32[4,32,256]{2,1,0:T(8,128)S(1)}, u32[]{:S(2)}, u32[]{:S(2)}) async-start(f32[4,32,256]{2,1,0:T(8,128)} %broadcast_in_dim.9), calls=%async_computation.2 | async-start | bytes 262144 | tf_op jit(solution)/shard_map/all_to_all | solution.py:336
  129.8 6.7 %inverse_factor.1.inverse_ref = f32[64,64]{1,0:T(8,128)} custom-call(f32[64,64]{1,0:T(8,128)} %copy-done.7), custom_call_target="tpu_custom_call" | custom-call | flops 1000 | bytes 1000 | tf_op jit(solution)/shard_map/inverse_factor/pallas_call | solution.py:168
  136.5 0.4 collective-permute-start.20
  137.0 0.2 collective-permute-start.16
  137.1 0.3 collective-permute-start.18
  137.5 0.2 collective-permute-start.17
  137.6 0.3 collective-permute-start.19
  138.0 0.7 broadcast_in_dim.20
  138.7 4.6 %all-to-all-start.3 = ((f32[8,32,256]{2,1,0:T(8,128)}), f32[8,32,256]{2,1,0:T(8,128)}, u32[]{:S(2)}, u32[]{:S(2)}) async-start(f32[8,32,256]{2,1,0:T(8,128)} %broadcast_in_dim.20), calls=%async_computation.3 | async-start | bytes 524288 | tf_op jit(solution)/shard_map/all_to_all | solution.py:344
  143.3 1.2 copy-done.4
  144.5 0.8 copy-done.5
  145.2 2.4 %orthonormal.1.basis_ref = bf16[3584,128]{1,0:T(8,128)(2,1)S(1)} custom-call(f32[64,64]{1,0:T(8,128)S(1)} %copy-done.5, f32[64,3584]{1,0:T(8,128)S(1)} %copy-done.4), custom_call_target="tpu_custom_call" | custom-call | flops 1000 | bytes 1000 | tf_op jit(solution)/shard_map/orthonormal/pallas_call | solution.py:183
  147.7 6.2 %input_gradient.1 = bf16[192,3584]{1,0:T(8,128)(2,1)} custom-call(s32[1]{0:T(128)} %bitcast.core_ref, bf16[192,256]{1,0:T(8,128)(2,1)S(1)} %get-tuple-element.61.grad_ref, bf16[3584,256]{1,0:T(8,128)(2,1)S(1)} %copy-done.2, bf16[1024,256]{1,0:T(8,128)(2,1)} %collective-permute-done.9.refs_0_, bf16[960,256]{1,0:T(8,128)(2,1)} %collective-permute-done.13.refs_1_, ...), custom_call_target="tpu_custom_call" | custom-call | flops 1000 | bytes 1000 | tf_op jit(solution)/shard_map/input_gradient/pallas_call | solution.py:263
  153.9 1.8 %all-to-all-done.3 = f32[8,32,256]{2,1,0:T(8,128)} async-done(((f32[8,32,256]{2,1,0:T(8,128)}), f32[8,32,256]{2,1,0:T(8,128)}, u32[]{:S(2)}, u32[]{:S(2)}) %all-to-all-start.3) | async-done | bytes 262176 | tf_op jit(solution)/shard_map/all_to_all | solution.py:344
  155.7 1.0 reduce_sum.29.mine_ref
  156.7 0.6 collective-permute-start.21
  157.3 0.9 collective-permute-done.21.other_ref
  158.1 2.0 %copy-done.1 = f32[3584,256]{1,0:T(8,128)S(1)} copy-done((f32[3584,256]{1,0:T(8,128)S(1)}, f32[3584,256]{1,0:T(8,128)}, u32[]{:S(2)}) %copy-start.1) | copy-done | bytes 3670040
  160.2 2.6 %finish.1 = (bf16[3584,256]{1,0:T(8,128)(2,1)}, f32[64,256]{1,0:T(8,128)}) custom-call(s32[1]{0:T(128)} %bitcast.core_ref, f32[32,256]{1,0:T(8,128)S(1)} %reduce_sum.29.mine_ref, f32[32,256]{1,0:T(8,128)S(1)} %collective-permute-done.21.other_ref, f32[64,64]{1,0:T(8,128)S(1)} %copy-done.6, bf16[3584,128]{1,0:T(8,128)(2,1)S(1)} %orthonormal.1.basis_ref, ...), custom_call_target="tpu_custom_call" | custom-call | flops 1000 | bytes 1000 | tf_op jit(solution)/shard_map/finish/pallas_call | solution.py:213
  (51 shorter events, 0.2 us)
Async XLA Ops:
  2.0 40.2 %copy-start.10 = (bf16[192,1792]{1,0:T(8,128)(2,1)}, bf16[192,1792]{1,0:T(8,128)(2,1)S(1)}, u32[]{:S(2)}) copy-start(bf16[192,1792]{1,0:T(8,128)(2,1)S(1)} %get-tuple-element.59.refs_0_) | copy-start | bytes 2064388
  2.0 45.0 %copy-start.9 = (bf16[192,1792]{1,0:T(8,128)(2,1)}, bf16[192,1792]{1,0:T(8,128)(2,1)S(1)}, u32[]{:S(2)}) copy-start(bf16[192,1792]{1,0:T(8,128)(2,1)S(1)} %get-tuple-element.60.refs_0_) | copy-start | bytes 2064388
  2.1 36.3 %copy-start.16 = (bf16[768,256]{1,0:T(8,128)(2,1)S(1)}, bf16[768,256]{1,0:T(8,128)(2,1)}, u32[]{:S(2)}) copy-start(bf16[768,256]{1,0:T(8,128)(2,1)} %param.6) | copy-start | bytes 1179652
  2.1 16.8 %collective-permute-start.5 = (bf16[192,1792]{1,0:T(8,128)(2,1)S(1)}, bf16[192,1792]{1,0:T(8,128)(2,1)S(1)}, u32[]{:S(2)}, u32[]{:S(2)}) collective-permute-start(bf16[192,1792]{1,0:T(8,128)(2,1)S(1)} %get-tuple-element.59.refs_0_), channel_id=1, source_target_pairs={{0,1},{1,2},{2,3},{3,0},{4,5},{5,6},{6,7},{7,4},{8,9},{9,10},{10,1... | collective-permute-start | bytes 2064392 | tf_op jit(solution)/shard_map/ppermute | solution.py:33
  4.3 16.9 %collective-permute-start.4 = (bf16[192,1792]{1,0:T(8,128)(2,1)S(1)}, bf16[192,1792]{1,0:T(8,128)(2,1)S(1)}, u32[]{:S(2)}, u32[]{:S(2)}) collective-permute-start(bf16[192,1792]{1,0:T(8,128)(2,1)S(1)} %get-tuple-element.59.refs_0_), channel_id=1, source_target_pairs={{0,3},{1,0},{2,1},{3,2},{4,7},{5,4},{6,5},{7,6},{8,11},{9,8},{10,9... | collective-permute-start | bytes 2064392 | tf_op jit(solution)/shard_map/ppermute | solution.py:33
  5.8 27.8 %collective-permute-start.1 = (bf16[192,1792]{1,0:T(8,128)(2,1)S(1)}, bf16[192,1792]{1,0:T(8,128)(2,1)S(1)}, u32[]{:S(2)}, u32[]{:S(2)}) collective-permute-start(bf16[192,1792]{1,0:T(8,128)(2,1)S(1)} %get-tuple-element.60.refs_0_), channel_id=1, source_target_pairs={{0,1},{1,2},{2,3},{3,0},{4,5},{5,6},{6,7},{7,4},{8,9},{9,10},{10,1... | collective-permute-start | bytes 2064392 | tf_op jit(solution)/shard_map/ppermute | solution.py:33
  5.8 30.1 %collective-permute-start = (bf16[192,1792]{1,0:T(8,128)(2,1)S(1)}, bf16[192,1792]{1,0:T(8,128)(2,1)S(1)}, u32[]{:S(2)}, u32[]{:S(2)}) collective-permute-start(bf16[192,1792]{1,0:T(8,128)(2,1)S(1)} %get-tuple-element.60.refs_0_), channel_id=1, source_target_pairs={{0,3},{1,0},{2,1},{3,2},{4,7},{5,4},{6,5},{7,6},{8,11},{9,8},{10,9... | collective-permute-start | bytes 2064392 | tf_op jit(solution)/shard_map/ppermute | solution.py:33
  18.8 17.1 %copy-start.14 = (bf16[192,1792]{1,0:T(8,128)(2,1)}, bf16[192,1792]{1,0:T(8,128)(2,1)S(1)}, u32[]{:S(2)}) copy-start(bf16[192,1792]{1,0:T(8,128)(2,1)S(1)} %collective-permute-done.5.refs_4_) | copy-start | bytes 2064388
  19.6 21.4 %collective-permute-start.6 = (bf16[96,1792]{1,0:T(8,128)(2,1)}, bf16[96,1792]{1,0:T(8,128)(2,1)}, u32[]{:S(2)}, u32[]{:S(2)}) collective-permute-start(bf16[96,1792]{1,0:T(8,128)(2,1)} %slice.50), channel_id=1, source_target_pairs={{0,1},{1,2},{2,3},{3,0},{4,5},{5,6},{6,7},{7,4},{8,9},{9,10},{10,1... | collective-permute-start | bytes 1032200 | tf_op jit(solution)/shard_map/ppermute | solution.py:33
  21.2 15.5 %copy-start.15 = (bf16[192,1792]{1,0:T(8,128)(2,1)}, bf16[192,1792]{1,0:T(8,128)(2,1)S(1)}, u32[]{:S(2)}) copy-start(bf16[192,1792]{1,0:T(8,128)(2,1)S(1)} %collective-permute-done.4.refs_1_) | copy-start | bytes 2064388
  22.0 20.2 %collective-permute-start.7 = (bf16[96,1792]{1,0:T(8,128)(2,1)}, bf16[96,1792]{1,0:T(8,128)(2,1)}, u32[]{:S(2)}, u32[]{:S(2)}) collective-permute-start(bf16[96,1792]{1,0:T(8,128)(2,1)} %slice.51), channel_id=1, source_target_pairs={{0,3},{1,0},{2,1},{3,2},{4,7},{5,4},{6,5},{7,6},{8,11},{9,8},{10,9... | collective-permute-start | bytes 1032200 | tf_op jit(solution)/shard_map/ppermute | solution.py:33
  33.6 13.5 %copy-start.12 = (bf16[192,1792]{1,0:T(8,128)(2,1)}, bf16[192,1792]{1,0:T(8,128)(2,1)S(1)}, u32[]{:S(2)}) copy-start(bf16[192,1792]{1,0:T(8,128)(2,1)S(1)} %collective-permute-done.1.refs_4_) | copy-start | bytes 2064388
  34.4 14.0 %collective-permute-start.2 = (bf16[96,1792]{1,0:T(8,128)(2,1)}, bf16[96,1792]{1,0:T(8,128)(2,1)}, u32[]{:S(2)}, u32[]{:S(2)}) collective-permute-start(bf16[96,1792]{1,0:T(8,128)(2,1)} %slice.48), channel_id=1, source_target_pairs={{0,1},{1,2},{2,3},{3,0},{4,5},{5,6},{6,7},{7,4},{8,9},{9,10},{10,1... | collective-permute-start | bytes 1032200 | tf_op jit(solution)/shard_map/ppermute | solution.py:33
  35.9 11.1 %copy-start.13 = (bf16[192,1792]{1,0:T(8,128)(2,1)}, bf16[192,1792]{1,0:T(8,128)(2,1)S(1)}, u32[]{:S(2)}) copy-start(bf16[192,1792]{1,0:T(8,128)(2,1)S(1)} %collective-permute-done.refs_1_) | copy-start | bytes 2064388
  36.7 12.9 %collective-permute-start.3 = (bf16[96,1792]{1,0:T(8,128)(2,1)}, bf16[96,1792]{1,0:T(8,128)(2,1)}, u32[]{:S(2)}, u32[]{:S(2)}) collective-permute-start(bf16[96,1792]{1,0:T(8,128)(2,1)} %slice.49), channel_id=1, source_target_pairs={{0,3},{1,0},{2,1},{3,2},{4,7},{5,4},{6,5},{7,6},{8,11},{9,8},{10,9... | collective-permute-start | bytes 1032200 | tf_op jit(solution)/shard_map/ppermute | solution.py:33
  49.6 7.5 %copy-start.2 = (bf16[3584,256]{1,0:T(8,128)(2,1)S(1)}, bf16[3584,256]{1,0:T(8,128)(2,1)}, u32[]{:S(2)}) copy-start(bf16[3584,256]{1,0:T(8,128)(2,1)} %weight_ref.1) | copy-start | bytes 5505028
  49.6 7.5 %copy-start.8 = (bf16[768,256]{1,0:T(8,128)(2,1)S(1)}, bf16[768,256]{1,0:T(8,128)(2,1)}, u32[]{:S(2)}) copy-start(bf16[768,256]{1,0:T(8,128)(2,1)} %fusion.refs_5_) | copy-start | bytes 1179652
  54.5 4.2 %copy-start.11 = (f32[8,4,7,4,128]{4,3,2,1,0:T(4,128)S(1)}, f32[8,4,7,4,128]{4,3,2,1,0:T(4,128)}, u32[]{:S(2)}) copy-start(f32[8,4,7,4,128]{4,3,2,1,0:T(4,128)} %get-tuple-element.34) | copy-start | bytes 1376260
  54.5 4.2 %collective-permute-start.8 = (f32[8,4,7,4,128]{4,3,2,1,0:T(4,128)}, f32[8,4,7,4,128]{4,3,2,1,0:T(4,128)S(1)}, u32[]{:S(2)}, u32[]{:S(2)}) collective-permute-start(f32[8,4,7,4,128]{4,3,2,1,0:T(4,128)} %get-tuple-element.35), channel_id=1, source_target_pairs={{0,4},{4,0},{1,5},{5,1},{2,6},{6,2},{3,7},{7,3},{8,12},{12,8},{9,1... | collective-permute-start | bytes 1376264 | tf_op jit(solution)/shard_map/ppermute | solution.py:33
  59.6 26.2 %all-to-all-start = ((f32[32,7,4,128]{3,2,1,0:T(4,128)}), f32[32,7,4,128]{3,2,1,0:T(4,128)S(1)}, u32[]{:S(2)}, u32[]{:S(2)}) async-start(f32[32,7,4,128]{3,2,1,0:T(4,128)} %bitcast.3), calls=%async_computation | async-start | bytes 917504 | tf_op jit(solution)/shard_map/all_to_all | solution.py:315
  71.5 14.4 %collective-permute-start.10 = (bf16[1024,256]{1,0:T(8,128)(2,1)S(1)}, bf16[1024,256]{1,0:T(8,128)(2,1)S(1)}, u32[]{:S(2)}, u32[]{:S(2)}) collective-permute-start(bf16[1024,256]{1,0:T(8,128)(2,1)S(1)} %constant_dynamic-slice_fusion), channel_id=1, source_target_pairs={{0,3},{1,0},{2,1},{3,2},{4,7},{5,4},{6,5},{7,6},{8,11},{9,8},{10,9... | collective-permute-start | bytes 1572872 | tf_op jit(solution)/shard_map/ppermute | solution.py:33
  74.2 13.8 %collective-permute-start.9 = (bf16[1024,256]{1,0:T(8,128)(2,1)S(1)}, bf16[1024,256]{1,0:T(8,128)(2,1)}, u32[]{:S(2)}, u32[]{:S(2)}) collective-permute-start(bf16[1024,256]{1,0:T(8,128)(2,1)S(1)} %constant_dynamic-slice_fusion), channel_id=1, source_target_pairs={{0,1},{1,2},{2,3},{3,0},{4,5},{5,6},{6,7},{7,4},{8,9},{9,10},{10,1... | collective-permute-start | bytes 1572872 | tf_op jit(solution)/shard_map/ppermute | solution.py:33
  88.8 22.4 %all-to-all-start.1 = ((f32[32,7,4,128]{3,2,1,0:T(4,128)}), f32[32,7,4,128]{3,2,1,0:T(4,128)S(1)}, u32[]{:S(2)}, u32[]{:S(2)}) async-start(f32[32,7,4,128]{3,2,1,0:T(4,128)} %broadcast_in_dim.8), calls=%async_computation.1 | async-start | bytes 917504 | tf_op jit(solution)/shard_map/all_to_all | solution.py:326
  97.8 38.7 %collective-permute-start.15 = (bf16[1984,256]{1,0:T(8,128)(2,1)}, bf16[1984,256]{1,0:T(8,128)(2,1)}, u32[]{:S(2)}, u32[]{:S(2)}) collective-permute-start(bf16[1984,256]{1,0:T(8,128)(2,1)} %pad_maximum_fusion), channel_id=1, source_target_pairs={{0,2},{1,3},{2,0},{3,1},{4,6},{5,7},{6,4},{7,5},{8,10},{9,11},{10,... | collective-permute-start | bytes 3047432 | tf_op jit(solution)/shard_map/ppermute | solution.py:33
  111.2 7.0 %collective-permute-start.11 = (f32[8,4,7,4,128]{4,3,2,1,0:T(4,128)S(1)}, f32[8,4,7,4,128]{4,3,2,1,0:T(4,128)S(1)}, u32[]{:S(2)}, u32[]{:S(2)}) collective-permute-start(f32[8,4,7,4,128]{4,3,2,1,0:T(4,128)S(1)} %bitcast.7), channel_id=1, source_target_pairs={{0,4},{4,0},{1,5},{5,1},{2,6},{6,2},{3,7},{7,3},{8,12},{12,8},{9,1... | collective-permute-start | bytes 1376264 | tf_op jit(solution)/shard_map/ppermute | solution.py:33
  115.5 21.0 %collective-permute-start.13 = (bf16[960,256]{1,0:T(8,128)(2,1)}, bf16[960,256]{1,0:T(8,128)(2,1)}, u32[]{:S(2)}, u32[]{:S(2)}) collective-permute-start(bf16[960,256]{1,0:T(8,128)(2,1)} %get-tuple-element.42), channel_id=1, source_target_pairs={{0,1},{1,2},{2,3},{3,0},{4,5},{5,6},{6,7},{7,4},{8,9},{9,10},{10,1... | collective-permute-start | bytes 1474568 | tf_op jit(solution)/shard_map/ppermute | solution.py:33
  115.5 21.0 %collective-permute-start.14 = (bf16[960,256]{1,0:T(8,128)(2,1)}, bf16[960,256]{1,0:T(8,128)(2,1)}, u32[]{:S(2)}, u32[]{:S(2)}) collective-permute-start(bf16[960,256]{1,0:T(8,128)(2,1)} %get-tuple-element.44), channel_id=1, source_target_pairs={{0,3},{1,0},{2,1},{3,2},{4,7},{5,4},{6,5},{7,6},{8,11},{9,8},{10,9... | collective-permute-start | bytes 1474568 | tf_op jit(solution)/shard_map/ppermute | solution.py:33
  118.2 2.0 %copy-start = (f32[3584,256]{1,0:T(8,128)S(1)}, f32[3584,256]{1,0:T(8,128)}, u32[]{:S(2)}) copy-start(f32[3584,256]{1,0:T(8,128)} %get-tuple-element.38.merged_ref) | copy-start | bytes 11010052
  122.8 0.9 copy-start.3
  123.7 0.6 copy-start.7
  124.3 1.4 collective-permute-start.12
  126.4 10.1 %all-to-all-start.2 = ((f32[4,32,256]{2,1,0:T(8,128)}), f32[4,32,256]{2,1,0:T(8,128)S(1)}, u32[]{:S(2)}, u32[]{:S(2)}) async-start(f32[4,32,256]{2,1,0:T(8,128)} %broadcast_in_dim.9), calls=%async_computation.2 | async-start | bytes 262144 | tf_op jit(solution)/shard_map/all_to_all | solution.py:336
  136.5 11.1 %collective-permute-start.20 = (bf16[1984,256]{1,0:T(8,128)(2,1)}, bf16[1984,256]{1,0:T(8,128)(2,1)}, u32[]{:S(2)}, u32[]{:S(2)}) collective-permute-start(bf16[1984,256]{1,0:T(8,128)(2,1)} %collective-permute-done.15.refs_4_), channel_id=1, source_target_pairs={{0,4},{4,0},{1,5},{5,1},{2,6},{6,2},{3,7},{7,3},{8,12},{12,8},{9,1... | collective-permute-start | bytes 3047432 | tf_op jit(solution)/shard_map/ppermute | solution.py:33
  137.0 10.7 %collective-permute-start.16 = (bf16[1024,256]{1,0:T(8,128)(2,1)}, bf16[1024,256]{1,0:T(8,128)(2,1)}, u32[]{:S(2)}, u32[]{:S(2)}) collective-permute-start(bf16[1024,256]{1,0:T(8,128)(2,1)} %collective-permute-done.9.refs_0_), channel_id=1, source_target_pairs={{0,4},{4,0},{1,5},{5,1},{2,6},{6,2},{3,7},{7,3},{8,12},{12,8},{9,1... | collective-permute-start | bytes 1572872 | tf_op jit(solution)/shard_map/ppermute | solution.py:33
  137.1 10.5 %collective-permute-start.18 = (bf16[1024,256]{1,0:T(8,128)(2,1)S(1)}, bf16[1024,256]{1,0:T(8,128)(2,1)}, u32[]{:S(2)}, u32[]{:S(2)}) collective-permute-start(bf16[1024,256]{1,0:T(8,128)(2,1)S(1)} %collective-permute-done.10.refs_2_), channel_id=1, source_target_pairs={{0,4},{4,0},{1,5},{5,1},{2,6},{6,2},{3,7},{7,3},{8,12},{12,8},{9,1... | collective-permute-start | bytes 1572872 | tf_op jit(solution)/shard_map/ppermute | solution.py:33
  137.5 10.1 %collective-permute-start.17 = (bf16[960,256]{1,0:T(8,128)(2,1)}, bf16[960,256]{1,0:T(8,128)(2,1)}, u32[]{:S(2)}, u32[]{:S(2)}) collective-permute-start(bf16[960,256]{1,0:T(8,128)(2,1)} %collective-permute-done.13.refs_1_), channel_id=1, source_target_pairs={{0,4},{4,0},{1,5},{5,1},{2,6},{6,2},{3,7},{7,3},{8,12},{12,8},{9,1... | collective-permute-start | bytes 1474568 | tf_op jit(solution)/shard_map/ppermute | solution.py:33
  137.6 10.0 %collective-permute-start.19 = (bf16[960,256]{1,0:T(8,128)(2,1)}, bf16[960,256]{1,0:T(8,128)(2,1)}, u32[]{:S(2)}, u32[]{:S(2)}) collective-permute-start(bf16[960,256]{1,0:T(8,128)(2,1)} %collective-permute-done.14.refs_3_), channel_id=1, source_target_pairs={{0,4},{4,0},{1,5},{5,1},{2,6},{6,2},{3,7},{7,3},{8,12},{12,8},{9,1... | collective-permute-start | bytes 1474568 | tf_op jit(solution)/shard_map/ppermute | solution.py:33
  138.7 17.0 %all-to-all-start.3 = ((f32[8,32,256]{2,1,0:T(8,128)}), f32[8,32,256]{2,1,0:T(8,128)}, u32[]{:S(2)}, u32[]{:S(2)}) async-start(f32[8,32,256]{2,1,0:T(8,128)} %broadcast_in_dim.20), calls=%async_computation.3 | async-start | bytes 524288 | tf_op jit(solution)/shard_map/all_to_all | solution.py:344
  143.3 1.2 copy-start.4
  144.5 0.8 copy-start.5
  147.7 10.5 %copy-start.6 = (f32[64,64]{1,0:T(8,128)S(1)}, f32[64,64]{1,0:T(8,128)}, u32[]{:S(2)}) copy-start(f32[64,64]{1,0:T(8,128)} %inverse_factor.1.inverse_ref) | copy-start | bytes 49156
  156.7 1.4 collective-permute-start.21
  158.1 2.0 %copy-start.1 = (f32[3584,256]{1,0:T(8,128)S(1)}, f32[3584,256]{1,0:T(8,128)}, u32[]{:S(2)}) copy-start(f32[3584,256]{1,0:T(8,128)} %get-tuple-element.38.merged_ref) | copy-start | bytes 11010052

commit v2 on v1

--- a/solution.py
+++ b/solution.py
@@ -12,7 +12,8 @@
 REPLICAS = 64
 STEP = 896
 TILES = (8, 4, 7, 4, 128)
-HALF_FEATURES, FIRST = FEATURES // 2, 1024
+HALF_FEATURES = FEATURES // 2
+PIVOTS = 8
 PLANE = ("z", "x")
 SMALL = pl.CostEstimate(flops=1000, bytes_accessed=1000, transcendentals=0)
 VMEM = pltpu.CompilerParams(vmem_limit_bytes=40 * 2**20)
@@ -51,9 +52,7 @@
     return first[:rows] + (first[rows : 2 * rows] + second[:rows] + small)
 
 
-def merged_and_left(core, pieces, grads, error, right, offset, before):
-    chunk = pieces[0].shape[1]
-    first = offset // STEP
+def merged_and_left(core, pieces, grads, error, right):
     count = len(pieces)
 
     def body(core_ref, *refs):
@@ -74,26 +73,23 @@
                 mine_ref[row, 0, lane] = mine[tile]
                 other_ref[row, 0, lane] = other[tile]
 
-    aliased = [] if before is None else list(before)
-    tiles = pl.BlockSpec((8, 1, 7, 4, 128), lambda i: (0, first + i, 0, 0, 0))
-    return pl.pallas_call(
-        body,
-        grid=(chunk // STEP,),
+    tiles = pl.BlockSpec((8, 1, 7, 4, 128), lambda i: (0, i, 0, 0, 0))
+    return pl.pallas_call(
+        body,
+        grid=(FEATURES // STEP,),
         in_specs=[pl.BlockSpec(memory_space=pltpu.SMEM)]
         + [pl.BlockSpec((piece.shape[0], STEP), lambda i: (0, i)) for piece in pieces]
-        + [whole(grads), pl.BlockSpec((STEP, COLUMNS), lambda i: (first + i, 0)), whole(right)]
-        + [pl.BlockSpec(memory_space=pl.ANY) for _ in aliased],
-        out_specs=[pl.BlockSpec((STEP, COLUMNS), lambda i: (first + i, 0)), tiles, tiles],
+        + [whole(grads), pl.BlockSpec((STEP, COLUMNS), lambda i: (i, 0)), whole(right)],
+        out_specs=[pl.BlockSpec((STEP, COLUMNS), lambda i: (i, 0)), tiles, tiles],
         out_shape=[
             jax.ShapeDtypeStruct((FEATURES, COLUMNS), F32),
             jax.ShapeDtypeStruct(TILES, F32),
             jax.ShapeDtypeStruct(TILES, F32),
         ],
-        input_output_aliases={4 + count + at: at for at in range(len(aliased))},
         compiler_params=ALL_VMEM,
         cost_estimate=SMALL,
         name="merged_and_left",
-    )(core, *pieces, grads, error, right, *aliased)
+    )(core, *pieces, grads, error, right)
 
 
 def ordered(core, mine, other):
@@ -154,14 +150,39 @@
 
 def inverse_factor(gram):
     def body(gram_ref, inverse_ref):
+        shape = (PIVOTS, 2 * RANK)
         rows = lax.broadcasted_iota(jnp.int32, (RANK, 2 * RANK), 0)
         lanes = lax.broadcasted_iota(jnp.int32, (RANK, 2 * RANK), 1)
         work = jnp.concatenate([gram_ref[...], jnp.zeros((RANK, RANK), F32)], 1)
         work = jnp.where(lanes == rows + RANK, 1.0, work)
-        for at in range(RANK):
-            pivot_row = work[at : at + 1, :]
-            factor = work[:, at : at + 1] * (1.0 / pivot_row[:, at : at + 1])
-            work = jnp.where(rows > at, work - factor * pivot_row, work)
+        tiles = [work[at : at + PIVOTS] for at in range(0, RANK, PIVOTS)]
+        local = lax.broadcasted_iota(jnp.int32, shape, 0)
+        for at in range(len(tiles)):
+            columns = [
+                [
+                    jnp.broadcast_to(tile[:, at * PIVOTS + k : at * PIVOTS + k + 1], shape)
+                    for tile in tiles[at:]
+                ]
+                for k in range(PIVOTS)
+            ]
+            pivot_rows = [tiles[at][k : k + 1] for k in range(PIVOTS)]
+            updates = [0.0] * len(tiles[at:])
+            for k in range(PIVOTS):
+                inverse = 1.0 / columns[k][0][k : k + 1]
+                scaled = pivot_rows[k] * inverse
+                for later in range(k + 1, PIVOTS):
+                    pivot_rows[later] -= columns[k][0][later : later + 1] * scaled
+                    factor = columns[later][0][k : k + 1] * inverse
+                    columns[later] = [
+                        column - done * factor
+                        for column, done in zip(columns[later], columns[k])
+                    ]
+                updates = [update + done * scaled for update, done in zip(updates, columns[k])]
+            for k in range(1, PIVOTS):
+                tiles[at] = jnp.where(local == k, pivot_rows[k], tiles[at])
+            for below in range(1, len(updates)):
+                tiles[at + below] = tiles[at + below] - updates[below]
+        work = jnp.concatenate(tiles, 0)
         pivots = jnp.sum(jnp.where(lanes == rows, work, 0.0), 1, keepdims=True)
         inverse_ref[...] = work[:, RANK:] * (1.0 / jnp.sqrt(pivots))
 
@@ -236,39 +257,62 @@
 def input_gradient(core, grads, weight, mine, other):
     def body(core_ref, grad_ref, weight_ref, *refs):
         *parcel_refs, out_ref = refs
-        before_high, far, after_high = parcel_refs[1], parcel_refs[4], parcel_refs[3]
-        blocks = [
-            grad_ref[...],
-            before_high[HALF_FEATURES - FIRST :, :],
-            far[HALF_FEATURES:, :],
-            after_high[HALF_FEATURES - FIRST :, :],
-        ]
-        for side in range(2):
-            half = core_ref[0] if side == 0 else 1 - core_ref[0]
-            before_low, before_high, after_low, after_high, far = parcel_refs[
-                5 * side : 5 * side + 5
+
+        def fill(halves):
+            for first in range(0, HALF_FEATURES, 896):
+                rows = slice(first, first + 896)
+                total = dot(grad_ref[...], weight_ref[rows, :], 1, 1)
+                for sent, weights in zip(parcel_refs, halves):
+                    total = total + dot(sent[HALF_FEATURES:, :], weights[rows, :], 1, 1)
+                out_ref[:, rows] = total.astype(BF16)
+
+        @pl.when(pl.program_id(0) == 0)
+        def _():
+            fill(parcel_refs[:3])
+
+        @pl.when(pl.program_id(0) == 1)
+        def _():
+            fill(parcel_refs[3:])
+
+    def half(side, core_ref):
+        return side + core_ref[0] * (1 - 2 * side)
+
+    vmem = pl.BlockSpec(memory_space=pltpu.VMEM)
+    return pl.pallas_call(
+        body,
+        grid_spec=pltpu.PrefetchScalarGridSpec(
+            num_scalar_prefetch=1,
+            grid=(2,),
+            in_specs=[
+                pl.BlockSpec((PART, COLUMNS), lambda side, core_ref: (0, 0)),
+                pl.BlockSpec(
+                    (HALF_FEATURES, COLUMNS), lambda side, core_ref: (half(side, core_ref), 0)
+                ),
             ]
-            for first, count, near in (
-                (0, FIRST, (before_low, after_low)),
-                (FIRST, HALF_FEATURES - FIRST, (before_high, after_high)),
-            ):
-                start = pl.multiple_of(half * HALF_FEATURES + first, 128)
-                total = dot(blocks[0], weight_ref[pl.ds(start, count), :], 1, 1)
-                total = total + dot(blocks[1], near[0][:count, :], 1, 1)
-                total = total + dot(blocks[2], far[first : first + count, :], 1, 1)
-                total = total + dot(blocks[3], near[1][:count, :], 1, 1)
-                out_ref[:, pl.ds(start, count)] = total.astype(BF16)
-
-    vmem = pl.BlockSpec(memory_space=pltpu.VMEM)
-    return pl.pallas_call(
-        body,
-        in_specs=[pl.BlockSpec(memory_space=pltpu.SMEM)] + [vmem] * 12,
-        out_specs=vmem,
+            + [vmem] * 6,
+            out_specs=pl.BlockSpec(
+                (PART, HALF_FEATURES), lambda side, core_ref: (0, half(side, core_ref))
+            ),
+        ),
         out_shape=jax.ShapeDtypeStruct((PART, FEATURES), BF16),
         compiler_params=VMEM,
         cost_estimate=SMALL,
         name="input_gradient",
     )(core, grads, weight, *mine, *other)
+
+
+def summed_copies(blocks, count):
+    def body(blocks_ref, copies_ref):
+        mean = jnp.sum(blocks_ref[...], 0) * (1 / REPLICAS)
+        copies_ref[...] = jnp.broadcast_to(mean[None], copies_ref.shape)
+
+    return pl.pallas_call(
+        body,
+        out_shape=jax.ShapeDtypeStruct((count, *blocks.shape[1:]), F32),
+        compiler_params=VMEM,
+        cost_estimate=SMALL,
+        name="summed_copies",
+    )(blocks)
 
 
 def both_ways(value):
@@ -286,43 +330,25 @@
     )
     right_rows = right_prev.T
 
-    cut = FEATURES // 2
-    chunks = [layer_input[:, :cut], layer_input[:, cut:]]
-    near = [both_ways(chunk) for chunk in chunks]
-    far = [
-        (shift(before[:96], "tensor", 4, 1), shift(after[96:], "tensor", 4, -1))
-        for before, after in near
+    low, high = layer_input[: PART // 2], layer_input[PART // 2 :]
+    before_low, after_high = shift(low, "tensor", 4, 1), shift(high, "tensor", 4, -1)
+    before_high, after_low = shift(high, "tensor", 4, 1), shift(low, "tensor", 4, -1)
+    far_low, far_high = shift(before_low, "tensor", 4, 1), shift(after_high, "tensor", 4, -1)
+    pieces = (layer_input, after_low, after_high, far_low, far_high, before_low, before_high)
+    merged, mine, other = merged_and_left(core_word, pieces, grads, error, right_rows)
+
+    half = lax.dynamic_slice_in_dim(query_weight, core * HALF_FEATURES, HALF_FEATURES, 0)
+    parcels = [
+        jnp.concatenate([half, grads[k * PART : (k + 1) * PART]], 0) for k in (1, 2, 3)
     ]
-    state = None
-    for at, chunk in enumerate(chunks):
-        before, after = near[at]
-        pieces = (chunk, after, *far[at], before)
-        state = merged_and_left(core_word, pieces, grads, error, right_rows, at * cut, state)
-    merged, mine, other = state
-
-    half = lax.dynamic_slice_in_dim(query_weight, core * HALF_FEATURES, HALF_FEATURES, 0)
-    low, high = half[:FIRST], half[FIRST:]
-    before, far_parcel, after = (
-        jnp.concatenate([rows, grads[k * PART : (k + 1) * PART]], 0)
-        for rows, k in ((high, 1), (half, 2), (high, 3))
-    )
-    low, before, far_parcel, after = lax.optimization_barrier(
-        (low, before, far_parcel, after, near[1][0])
-    )[:4]
-    lows = both_ways(low)
+    parcels = lax.optimization_barrier((*parcels, before_high))[:3]
+    before, after = shift(parcels[0], "tensor", 4, 1), shift(parcels[2], "tensor", 4, -1)
 
     total = (mine + shift(other, "c", 2, 1)).reshape(32, 7, 4, 128)
     blocks = lax.all_to_all(total, PLANE, 0, 0, tiled=True)
-    reduced = jnp.sum(blocks, 0) * (1 / REPLICAS)
-    reduced, *lows = lax.optimization_barrier((reduced, *lows))
-    parcels = (
-        lows[0],
-        shift(before, "tensor", 4, 1),
-        lows[1],
-        shift(after, "tensor", 4, -1),
-        shift(far_parcel, "tensor", 4, 2),
-    )
-    copies = jnp.broadcast_to(reduced, (32, 7, 4, 128))
+    blocks, before, after = lax.optimization_barrier((blocks, before, after))
+    parcels = (before, shift(parcels[1], "tensor", 4, 2), after)
+    copies = summed_copies(blocks, 32)
     mine = lax.all_to_all(copies, PLANE, 0, 0, tiled=True).reshape(TILES)
     other = shift(mine, "c", 2, 1)
 

time: 164 us -> 160 us (0.976)
  waiting for transfers between devices: 56.1 us -> 70.1 us
  starting transfers between devices: 55.3 us -> 47.7 us
  Pallas kernels: 30.2 us -> 25.3 us
  local copies, waits for them, and re-layouts: 14.6 us -> 11.4 us
  other arithmetic: 5.82 us -> 4.15 us
    ppermute x22 -> x16, waiting for transfers between devices: 29.3 us -> 50.7 us  [shift(): lax.ppermute(value, axis, [(at, (at + by) % size) for at in range(size)])]
    all_to_all x1, waiting for transfers between devices: 11.6 us -> 3.79 us  [shards(): blocks = lax.all_to_all(total, PLANE, 0, 0, tiled=True)]
    ppermute x22 -> x16, starting transfers between devices: 27.8 us -> 22.7 us  [shift(): lax.ppermute(value, axis, [(at, (at + by) % size) for at in range(size)])]
    pallas_call x1, Pallas kernels: 6.72 us -> 3.01 us  [inverse_factor(): pl.pallas_call(body, out_shape=jax.ShapeDtypeStruct((RANK, RANK), F32), c...]
    slice x7 -> x1, local copies, waits for them, and re-layouts: 4.66 us -> 2.4 us  [shards(): low, high = (layer_input[:PART // 2], layer_input[PART // 2:])]
    all_to_all x1, waiting for transfers between devices: 0.01 us -> 1.78 us  [shards(): mine = jnp.sum(lax.all_to_all(copies, 'x', 0, 0, tiled=True), 0)]
    all_to_all x1, starting transfers between devices: 8.92 us -> 7.24 us  [shards(): mine = lax.all_to_all(copies, PLANE, 0, 0, tiled=True).reshape(TILES)]
    unnamed x34 -> x22, local copies, waits for them, and re-layouts: 7.59 us -> 7.56 us
  transfers between devices with their start and end apart: 26 -> 20, of which waited for: 13 -> 13; matrix products, arithmetic and copies ran while one was open for 5% -> 4% of each run, Pallas kernels for 14% -> 9%
where the time goes in v2:
time: 160 us
  waiting for transfers between devices  70.1 us (44%)
  starting transfers between devices  47.7 us (30%)
  Pallas kernels  25.3 us (16%)
  local copies, waits for them, and re-layouts  11.4 us (7%)
  other arithmetic  4.15 us (3%)
    ppermute x16, waiting for transfers between devices, shift(): lax.ppermute(value, axis, [(at, (at + by) % size) for at in range(size)])  50.7 us
    ppermute x16, starting transfers between devices, shift(): lax.ppermute(value, axis, [(at, (at + by) % size) for at in range(size)])  22.7 us
    all_to_all x1, waiting for transfers between devices, shards(): mine = lax.all_to_all(copies, PLANE, 0, 0, tiled=True).reshape(TILES)  12.2 us
    all_to_all x1, starting transfers between devices, shards(): blocks = lax.all_to_all(total, PLANE, 0, 0, tiled=True)  11 us
    pallas_call x1, Pallas kernels, merged_and_left(): pl.pallas_call(body, grid=(FEATURES // STEP,), in_specs=[pl.BlockSpec(mem...  7.66 us
    unnamed x22, local copies, waits for them, and re-layouts  7.56 us
    all_to_all x1, starting transfers between devices, shards(): mine = lax.all_to_all(copies, PLANE, 0, 0, tiled=True).reshape(TILES)  7.24 us
    pallas_call x1, Pallas kernels, input_gradient(): pl.pallas_call(body, grid_spec=pltpu.PrefetchScalarGridSpec(num_scalar_pr...  6.23 us
  transfers between devices with their start and end apart: 20, of which 13 were waited for; matrix products, arithmetic and copies ran while one was open for 4% of the time, Pallas kernels for 9%

profile of v2, /device:TPU:1, one launch (start us, length us, event | category | flops | bytes accessed | tf_op | source)
XLA Modules:
  0.0 159.5 jit_solution(3132559714128284608)
XLA Ops:
  0.7 2.4 %fusion.1 = (bf16[96,3584]{1,0:T(8,128)(2,1)}, bf16[96,3584]{1,0:T(8,128)(2,1)S(1)}) fusion(bf16[192,3584]{1,0:T(8,128)(2,1)} %refs_0_.1), kind=kLoop, calls=%fused_computation.9 | loop fusion | bytes 2752512 | tf_op jit(solution)/shard_map/slice | solution.py:333
  3.0 2.1 %collective-permute-start.2 = (bf16[96,3584]{1,0:T(8,128)(2,1)S(1)}, bf16[96,3584]{1,0:T(8,128)(2,1)}, u32[]{:S(2)}, u32[]{:S(2)}) collective-permute-start(bf16[96,3584]{1,0:T(8,128)(2,1)S(1)} %get-tuple-element.48), channel_id=1, source_target_pairs={{0,1},{1,2},{2,3},{3,0},{4,5},{5,6},{6,7},{7,4},{8,9},{9,10},{10,1... | collective-permute-start | bytes 2064392 | tf_op jit(solution)/shard_map/ppermute | solution.py:34
  5.2 1.4 collective-permute-start.1
  6.6 0.0 collective-permute-start.5
  6.6 2.7 %collective-permute-start = (bf16[96,3584]{1,0:T(8,128)(2,1)S(1)}, bf16[96,3584]{1,0:T(8,128)(2,1)}, u32[]{:S(2)}, u32[]{:S(2)}) collective-permute-start(bf16[96,3584]{1,0:T(8,128)(2,1)S(1)} %get-tuple-element.48), channel_id=1, source_target_pairs={{0,3},{1,0},{2,1},{3,2},{4,7},{5,4},{6,5},{7,6},{8,11},{9,8},{10,9... | collective-permute-start | bytes 2064392 | tf_op jit(solution)/shard_map/ppermute | solution.py:34
  9.3 10.5 %collective-permute-done.2.refs_5_ = bf16[96,3584]{1,0:T(8,128)(2,1)} collective-permute-done((bf16[96,3584]{1,0:T(8,128)(2,1)S(1)}, bf16[96,3584]{1,0:T(8,128)(2,1)}, u32[]{:S(2)}, u32[]{:S(2)}) %collective-permute-start.2) | collective-permute-done | bytes 688160 | tf_op jit(solution)/shard_map/ppermute | solution.py:34
  19.8 1.6 collective-permute-start.3
  21.4 0.0 collective-permute-done.1.refs_2_
  21.4 1.6 %collective-permute-start.4 = (bf16[96,3584]{1,0:T(8,128)(2,1)}, bf16[96,3584]{1,0:T(8,128)(2,1)}, u32[]{:S(2)}, u32[]{:S(2)}) collective-permute-start(bf16[96,3584]{1,0:T(8,128)(2,1)} %collective-permute-done.1.refs_2_), channel_id=1, source_target_pairs={{0,3},{1,0},{2,1},{3,2},{4,7},{5,4},{6,5},{7,6},{8,11},{9,8},{10,9... | collective-permute-start | bytes 2064392 | tf_op jit(solution)/shard_map/ppermute | solution.py:34
  23.0 0.0 copy-done.10
  23.0 1.7 %fusion.refs_7_ = bf16[768,256]{1,0:T(8,128)(2,1)} fusion(s32[]{:T(128)S(6)} %select_n.12, bf16[768,256]{1,0:T(8,128)(2,1)S(1)} %copy-done.10), kind=kLoop, calls=%fused_computation.5 | loop fusion | flops 786432 | bytes 786436 | tf_op jit(solution)/shard_map/concatenate | solution.py:329
  24.8 0.1 constant_dynamic-slice_fusion.1
  24.8 9.7 %collective-permute-done.5.refs_6_ = bf16[96,3584]{1,0:T(8,128)(2,1)} collective-permute-done((bf16[96,3584]{1,0:T(8,128)(2,1)}, bf16[96,3584]{1,0:T(8,128)(2,1)}, u32[]{:S(2)}, u32[]{:S(2)}) %collective-permute-start.5) | collective-permute-done | bytes 688160 | tf_op jit(solution)/shard_map/ppermute | solution.py:34
  34.6 1.5 collective-permute-done.refs_1_
  36.0 13.3 %collective-permute-done.3.refs_3_ = bf16[96,3584]{1,0:T(8,128)(2,1)} collective-permute-done((bf16[96,3584]{1,0:T(8,128)(2,1)}, bf16[96,3584]{1,0:T(8,128)(2,1)}, u32[]{:S(2)}, u32[]{:S(2)}) %collective-permute-start.3) | collective-permute-done | bytes 688160 | tf_op jit(solution)/shard_map/ppermute | solution.py:34
  49.3 1.5 collective-permute-done.4.refs_4_
  50.8 7.7 %merged_and_left.1 = (f32[3584,256]{1,0:T(8,128)}, f32[8,4,7,4,128]{4,3,2,1,0:T(4,128)}, f32[8,4,7,4,128]{4,3,2,1,0:T(4,128)}) custom-call(s32[1]{0:T(128)} %bitcast.core_ref, bf16[192,3584]{1,0:T(8,128)(2,1)} %refs_0_.1, bf16[96,3584]{1,0:T(8,128)(2,1)} %collective-permute-done.refs_1_, bf16[96,3584]{1,0:T(8,128)(2,1)} %collective-permute-done.1.refs_2_, ...), custom_call_target="tpu_custom_call" | custom-call | flops 1000 | bytes 1000 | tf_op jit(solution)/shard_map/merged_and_left/pallas_call | solution.py:77
  58.5 2.1 %collective-permute-start.6 = (f32[8,4,7,4,128]{4,3,2,1,0:T(4,128)}, f32[8,4,7,4,128]{4,3,2,1,0:T(4,128)S(1)}, u32[]{:S(2)}, u32[]{:S(2)}) collective-permute-start(f32[8,4,7,4,128]{4,3,2,1,0:T(4,128)} %get-tuple-element.26), channel_id=1, source_target_pairs={{0,4},{4,0},{1,5},{5,1},{2,6},{6,2},{3,7},{7,3},{8,12},{12,8},{9,1... | collective-permute-start | bytes 1376264 | tf_op jit(solution)/shard_map/ppermute | solution.py:34
  60.6 0.0 copy-start.9
  60.6 1.5 pad_maximum_fusion.2
  62.1 1.3 collective-permute-start.7
  63.4 1.4 collective-permute-start.8
  64.8 0.0 collective-permute-done.6
  64.8 0.9 add.19
  65.7 11.0 %all-to-all-start = ((f32[32,7,4,128]{3,2,1,0:T(4,128)}), f32[32,7,4,128]{3,2,1,0:T(4,128)S(1)}, u32[]{:S(2)}, u32[]{:S(2)}) async-start(f32[32,7,4,128]{3,2,1,0:T(4,128)} %bitcast.3), calls=%async_computation | async-start | bytes 917504 | tf_op jit(solution)/shard_map/all_to_all | solution.py:348
  76.7 11.0 %collective-permute-done.7.refs_0_ = bf16[1984,256]{1,0:T(8,128)(2,1)} collective-permute-done((bf16[1984,256]{1,0:T(8,128)(2,1)}, bf16[1984,256]{1,0:T(8,128)(2,1)}, u32[]{:S(2)}, u32[]{:S(2)}) %collective-permute-start.7) | collective-permute-done | bytes 1015840 | tf_op jit(solution)/shard_map/ppermute | solution.py:34
  87.7 0.0 collective-permute-done.8.refs_2_
  87.7 3.8 %all-to-all-done.blocks_ref = f32[32,7,4,128]{3,2,1,0:T(4,128)S(1)} async-done(((f32[32,7,4,128]{3,2,1,0:T(4,128)}), f32[32,7,4,128]{3,2,1,0:T(4,128)S(1)}, u32[]{:S(2)}, u32[]{:S(2)}) %all-to-all-start) | async-done | bytes 458784 | tf_op jit(solution)/shard_map/all_to_all | solution.py:348
  91.5 0.9 summed_copies.1
  92.4 7.2 %all-to-all-start.1 = ((f32[32,7,4,128]{3,2,1,0:T(4,128)}), f32[32,7,4,128]{3,2,1,0:T(4,128)S(1)}, u32[]{:S(2)}, u32[]{:S(2)}) async-start(f32[32,7,4,128]{3,2,1,0:T(4,128)} %summed_copies.1), calls=%async_computation.1 | async-start | bytes 917504 | tf_op jit(solution)/shard_map/all_to_all | solution.py:352
  99.6 2.2 %collective-permute-start.11 = (bf16[1984,256]{1,0:T(8,128)(2,1)}, bf16[1984,256]{1,0:T(8,128)(2,1)}, u32[]{:S(2)}, u32[]{:S(2)}) collective-permute-start(bf16[1984,256]{1,0:T(8,128)(2,1)} %get-tuple-element.34), channel_id=1, source_target_pairs={{0,2},{1,3},{2,0},{3,1},{4,6},{5,7},{6,4},{7,5},{8,10},{9,11},{10,... | collective-permute-start | bytes 3047432 | tf_op jit(solution)/shard_map/ppermute | solution.py:34
  101.8 12.2 %all-to-all-done.1 = f32[32,7,4,128]{3,2,1,0:T(4,128)S(1)} async-done(((f32[32,7,4,128]{3,2,1,0:T(4,128)}), f32[32,7,4,128]{3,2,1,0:T(4,128)S(1)}, u32[]{:S(2)}, u32[]{:S(2)}) %all-to-all-start.1) | async-done | bytes 458784 | tf_op jit(solution)/shard_map/all_to_all | solution.py:352
  114.0 3.2 %collective-permute-start.9 = (f32[8,4,7,4,128]{4,3,2,1,0:T(4,128)S(1)}, f32[8,4,7,4,128]{4,3,2,1,0:T(4,128)S(1)}, u32[]{:S(2)}, u32[]{:S(2)}) collective-permute-start(f32[8,4,7,4,128]{4,3,2,1,0:T(4,128)S(1)} %bitcast.7), channel_id=1, source_target_pairs={{0,4},{4,0},{1,5},{5,1},{2,6},{6,2},{3,7},{7,3},{8,12},{12,8},{9,1... | collective-permute-start | bytes 1376264 | tf_op jit(solution)/shard_map/ppermute | solution.py:34
  117.2 1.4 collective-permute-done.9.other_ref
  118.6 2.0 %copy-done = f32[3584,256]{1,0:T(8,128)S(1)} copy-done((f32[3584,256]{1,0:T(8,128)S(1)}, f32[3584,256]{1,0:T(8,128)}, u32[]{:S(2)}) %copy-start) | copy-done | bytes 3670040
  120.7 2.5 %cross_and_gram.1 = (f32[64,3584]{1,0:T(8,128)S(1)}, f32[64,256]{1,0:T(8,128)S(1)}, f32[64,64]{1,0:T(8,128)S(1)}) custom-call(s32[1]{0:T(128)} %bitcast.core_ref, f32[8,4,7,4,128]{4,3,2,1,0:T(4,128)S(1)} %bitcast.8, f32[8,4,7,4,128]{4,3,2,1,0:T(4,128)S(1)} %collective-permute-done.9.other_ref, f32[3584,256]{1,0:T(8,128)S(1)} %copy-done), custom_call_target="tpu_custom_call" | custom-call | flops 1000 | bytes 1000 | tf_op jit(solution)/shard_map/cross_and_gram/pallas_call | solution.py:126
  123.2 0.0 copy-start.3
  123.2 0.9 copy-done.3
  124.1 0.6 copy-done.7
  124.8 0.4 collective-permute-start.10
  125.1 0.9 collective-permute-done.10
  126.0 0.7 broadcast_in_dim.6
  126.7 3.3 %all-to-all-start.2 = ((f32[4,32,256]{2,1,0:T(8,128)}), f32[4,32,256]{2,1,0:T(8,128)S(1)}, u32[]{:S(2)}, u32[]{:S(2)}) async-start(f32[4,32,256]{2,1,0:T(8,128)} %broadcast_in_dim.6), calls=%async_computation.2 | async-start | bytes 262144 | tf_op jit(solution)/shard_map/all_to_all | solution.py:362
  130.0 3.0 %inverse_factor.1.inverse_ref = f32[64,64]{1,0:T(8,128)} custom-call(f32[64,64]{1,0:T(8,128)} %copy-done.7), custom_call_target="tpu_custom_call" | custom-call | flops 1000 | bytes 1000 | tf_op jit(solution)/shard_map/inverse_factor/pallas_call | solution.py:189
  133.0 1.8 %all-to-all-done.2 = f32[4,32,256]{2,1,0:T(8,128)S(1)} async-done(((f32[4,32,256]{2,1,0:T(8,128)}), f32[4,32,256]{2,1,0:T(8,128)S(1)}, u32[]{:S(2)}, u32[]{:S(2)}) %all-to-all-start.2) | async-done | bytes 131104 | tf_op jit(solution)/shard_map/all_to_all | solution.py:362
  134.8 0.0 collective-permute-done.11.refs_1_
  134.8 1.7 %collective-permute-start.12 = (bf16[1984,256]{1,0:T(8,128)(2,1)}, bf16[1984,256]{1,0:T(8,128)(2,1)}, u32[]{:S(2)}, u32[]{:S(2)}) collective-permute-start(bf16[1984,256]{1,0:T(8,128)(2,1)} %collective-permute-done.7.refs_0_), channel_id=1, source_target_pairs={{0,4},{4,0},{1,5},{5,1},{2,6},{6,2},{3,7},{7,3},{8,12},{12,8},{9,1... | collective-permute-start | bytes 3047432 | tf_op jit(solution)/shard_map/ppermute | solution.py:34
  136.5 0.1 collective-permute-start.13
  136.6 0.4 collective-permute-start.14
  137.0 0.7 broadcast_in_dim.7
  137.7 3.4 %all-to-all-start.3 = ((f32[8,32,256]{2,1,0:T(8,128)}), f32[8,32,256]{2,1,0:T(8,128)S(1)}, u32[]{:S(2)}, u32[]{:S(2)}) async-start(f32[8,32,256]{2,1,0:T(8,128)} %broadcast_in_dim.7), calls=%async_computation.3 | async-start | bytes 524288 | tf_op jit(solution)/shard_map/all_to_all | solution.py:370
  141.2 0.0 copy-start.4
  141.2 1.2 copy-done.4
  142.3 0.8 copy-done.5
  143.1 2.4 %orthonormal.1.basis_ref = bf16[3584,128]{1,0:T(8,128)(2,1)S(1)} custom-call(f32[64,64]{1,0:T(8,128)S(1)} %copy-done.5, f32[64,3584]{1,0:T(8,128)S(1)} %copy-done.4), custom_call_target="tpu_custom_call" | custom-call | flops 1000 | bytes 1000 | tf_op jit(solution)/shard_map/orthonormal/pallas_call | solution.py:204
  145.5 0.0 collective-permute-done.12.refs_3_
  145.5 0.0 collective-permute-done.13.refs_4_
  145.5 0.0 collective-permute-done.14.refs_5_
  145.5 6.2 %input_gradient.1 = bf16[192,3584]{1,0:T(8,128)(2,1)} custom-call(s32[1]{0:T(128)} %bitcast.core_ref, bf16[192,256]{1,0:T(8,128)(2,1)S(1)} %get-tuple-element.52.grad_ref, bf16[3584,256]{1,0:T(8,128)(2,1)S(1)} %copy-done.2, bf16[1984,256]{1,0:T(8,128)(2,1)} %collective-permute-done.7.refs_0_, bf16[1984,256]{1,0:T(8,128)(2,1)} %collective-permute-done.11.refs_1_, ...), custom_call_target="tpu_custom_call" | custom-call | flops 1000 | bytes 1000 | tf_op jit(solution)/shard_map/input_gradient/pallas_call | solution.py:281
  151.8 1.7 %all-to-all-done.3 = f32[8,32,256]{2,1,0:T(8,128)S(1)} async-done(((f32[8,32,256]{2,1,0:T(8,128)}), f32[8,32,256]{2,1,0:T(8,128)S(1)}, u32[]{:S(2)}, u32[]{:S(2)}) %all-to-all-start.3) | async-done | bytes 262176 | tf_op jit(solution)/shard_map/all_to_all | solution.py:370
  153.5 0.5 collective-permute-start.15
  154.0 0.9 collective-permute-done.15.other_ref
  154.9 2.0 %copy-done.1 = f32[3584,256]{1,0:T(8,128)S(1)} copy-done((f32[3584,256]{1,0:T(8,128)S(1)}, f32[3584,256]{1,0:T(8,128)}, u32[]{:S(2)}) %copy-start.1) | copy-done | bytes 3670040
  156.9 2.6 %finish.1 = (bf16[3584,256]{1,0:T(8,128)(2,1)}, f32[64,256]{1,0:T(8,128)}) custom-call(s32[1]{0:T(128)} %bitcast.core_ref, f32[32,256]{1,0:T(8,128)S(1)} %reduce_sum.19.mine_ref, f32[32,256]{1,0:T(8,128)S(1)} %collective-permute-done.15.other_ref, f32[64,64]{1,0:T(8,128)S(1)} %copy-done.6, bf16[3584,128]{1,0:T(8,128)(2,1)S(1)} %orthonormal.1.basis_ref, ...), custom_call_target="tpu_custom_call" | custom-call | flops 1000 | bytes 1000 | tf_op jit(solution)/shard_map/finish/pallas_call | solution.py:234
  (17 shorter events, 0.1 us)
Async XLA Ops:
  0.6 22.4 %copy-start.10 = (bf16[768,256]{1,0:T(8,128)(2,1)S(1)}, bf16[768,256]{1,0:T(8,128)(2,1)}, u32[]{:S(2)}) copy-start(bf16[768,256]{1,0:T(8,128)(2,1)} %param.6) | copy-start | bytes 1179652
  0.6 24.1 %copy-start.2 = (bf16[3584,256]{1,0:T(8,128)(2,1)S(1)}, bf16[3584,256]{1,0:T(8,128)(2,1)}, u32[]{:S(2)}) copy-start(bf16[3584,256]{1,0:T(8,128)(2,1)} %weight_ref.1) | copy-start | bytes 5505028
  3.0 16.8 %collective-permute-start.2 = (bf16[96,3584]{1,0:T(8,128)(2,1)S(1)}, bf16[96,3584]{1,0:T(8,128)(2,1)}, u32[]{:S(2)}, u32[]{:S(2)}) collective-permute-start(bf16[96,3584]{1,0:T(8,128)(2,1)S(1)} %get-tuple-element.48), channel_id=1, source_target_pairs={{0,1},{1,2},{2,3},{3,0},{4,5},{5,6},{6,7},{7,4},{8,9},{9,10},{10,1... | collective-permute-start | bytes 2064392 | tf_op jit(solution)/shard_map/ppermute | solution.py:34
  5.2 16.2 %collective-permute-start.1 = (bf16[96,3584]{1,0:T(8,128)(2,1)}, bf16[96,3584]{1,0:T(8,128)(2,1)}, u32[]{:S(2)}, u32[]{:S(2)}) collective-permute-start(bf16[96,3584]{1,0:T(8,128)(2,1)} %get-tuple-element.47), channel_id=1, source_target_pairs={{0,3},{1,0},{2,1},{3,2},{4,7},{5,4},{6,5},{7,6},{8,11},{9,8},{10,9... | collective-permute-start | bytes 2064392 | tf_op jit(solution)/shard_map/ppermute | solution.py:34
  6.6 28.0 %collective-permute-start.5 = (bf16[96,3584]{1,0:T(8,128)(2,1)}, bf16[96,3584]{1,0:T(8,128)(2,1)}, u32[]{:S(2)}, u32[]{:S(2)}) collective-permute-start(bf16[96,3584]{1,0:T(8,128)(2,1)} %get-tuple-element.47), channel_id=1, source_target_pairs={{0,1},{1,2},{2,3},{3,0},{4,5},{5,6},{6,7},{7,4},{8,9},{9,10},{10,1... | collective-permute-start | bytes 2064392 | tf_op jit(solution)/shard_map/ppermute | solution.py:34
  6.6 29.4 %collective-permute-start = (bf16[96,3584]{1,0:T(8,128)(2,1)S(1)}, bf16[96,3584]{1,0:T(8,128)(2,1)}, u32[]{:S(2)}, u32[]{:S(2)}) collective-permute-start(bf16[96,3584]{1,0:T(8,128)(2,1)S(1)} %get-tuple-element.48), channel_id=1, source_target_pairs={{0,3},{1,0},{2,1},{3,2},{4,7},{5,4},{6,5},{7,6},{8,11},{9,8},{10,9... | collective-permute-start | bytes 2064392 | tf_op jit(solution)/shard_map/ppermute | solution.py:34
  19.8 29.5 %collective-permute-start.3 = (bf16[96,3584]{1,0:T(8,128)(2,1)}, bf16[96,3584]{1,0:T(8,128)(2,1)}, u32[]{:S(2)}, u32[]{:S(2)}) collective-permute-start(bf16[96,3584]{1,0:T(8,128)(2,1)} %collective-permute-done.2.refs_5_), channel_id=1, source_target_pairs={{0,1},{1,2},{2,3},{3,0},{4,5},{5,6},{6,7},{7,4},{8,9},{9,10},{10,1... | collective-permute-start | bytes 2064392 | tf_op jit(solution)/shard_map/ppermute | solution.py:34
  21.4 29.4 %collective-permute-start.4 = (bf16[96,3584]{1,0:T(8,128)(2,1)}, bf16[96,3584]{1,0:T(8,128)(2,1)}, u32[]{:S(2)}, u32[]{:S(2)}) collective-permute-start(bf16[96,3584]{1,0:T(8,128)(2,1)} %collective-permute-done.1.refs_2_), channel_id=1, source_target_pairs={{0,3},{1,0},{2,1},{3,2},{4,7},{5,4},{6,5},{7,6},{8,11},{9,8},{10,9... | collective-permute-start | bytes 2064392 | tf_op jit(solution)/shard_map/ppermute | solution.py:34
  50.8 9.8 %copy-start.8 = (bf16[768,256]{1,0:T(8,128)(2,1)S(1)}, bf16[768,256]{1,0:T(8,128)(2,1)}, u32[]{:S(2)}) copy-start(bf16[768,256]{1,0:T(8,128)(2,1)} %fusion.refs_7_) | copy-start | bytes 1179652
  58.5 6.3 %collective-permute-start.6 = (f32[8,4,7,4,128]{4,3,2,1,0:T(4,128)}, f32[8,4,7,4,128]{4,3,2,1,0:T(4,128)S(1)}, u32[]{:S(2)}, u32[]{:S(2)}) collective-permute-start(f32[8,4,7,4,128]{4,3,2,1,0:T(4,128)} %get-tuple-element.26), channel_id=1, source_target_pairs={{0,4},{4,0},{1,5},{5,1},{2,6},{6,2},{3,7},{7,3},{8,12},{12,8},{9,1... | collective-permute-start | bytes 1376264 | tf_op jit(solution)/shard_map/ppermute | solution.py:34
  60.6 4.2 %copy-start.9 = (f32[8,4,7,4,128]{4,3,2,1,0:T(4,128)S(1)}, f32[8,4,7,4,128]{4,3,2,1,0:T(4,128)}, u32[]{:S(2)}) copy-start(f32[8,4,7,4,128]{4,3,2,1,0:T(4,128)} %get-tuple-element.25) | copy-start | bytes 1376260
  62.1 25.6 %collective-permute-start.7 = (bf16[1984,256]{1,0:T(8,128)(2,1)}, bf16[1984,256]{1,0:T(8,128)(2,1)}, u32[]{:S(2)}, u32[]{:S(2)}) collective-permute-start(bf16[1984,256]{1,0:T(8,128)(2,1)} %get-tuple-element.27), channel_id=1, source_target_pairs={{0,1},{1,2},{2,3},{3,0},{4,5},{5,6},{6,7},{7,4},{8,9},{9,10},{10,1... | collective-permute-start | bytes 3047432 | tf_op jit(solution)/shard_map/ppermute | solution.py:34
  63.4 24.3 %collective-permute-start.8 = (bf16[1984,256]{1,0:T(8,128)(2,1)S(1)}, bf16[1984,256]{1,0:T(8,128)(2,1)}, u32[]{:S(2)}, u32[]{:S(2)}) collective-permute-start(bf16[1984,256]{1,0:T(8,128)(2,1)S(1)} %get-tuple-element.28), channel_id=1, source_target_pairs={{0,3},{1,0},{2,1},{3,2},{4,7},{5,4},{6,5},{7,6},{8,11},{9,8},{10,9... | collective-permute-start | bytes 3047432 | tf_op jit(solution)/shard_map/ppermute | solution.py:34
  65.7 25.8 %all-to-all-start = ((f32[32,7,4,128]{3,2,1,0:T(4,128)}), f32[32,7,4,128]{3,2,1,0:T(4,128)S(1)}, u32[]{:S(2)}, u32[]{:S(2)}) async-start(f32[32,7,4,128]{3,2,1,0:T(4,128)} %bitcast.3), calls=%async_computation | async-start | bytes 917504 | tf_op jit(solution)/shard_map/all_to_all | solution.py:348
  92.4 21.6 %all-to-all-start.1 = ((f32[32,7,4,128]{3,2,1,0:T(4,128)}), f32[32,7,4,128]{3,2,1,0:T(4,128)S(1)}, u32[]{:S(2)}, u32[]{:S(2)}) async-start(f32[32,7,4,128]{3,2,1,0:T(4,128)} %summed_copies.1), calls=%async_computation.1 | async-start | bytes 917504 | tf_op jit(solution)/shard_map/all_to_all | solution.py:352
  99.6 35.2 %collective-permute-start.11 = (bf16[1984,256]{1,0:T(8,128)(2,1)}, bf16[1984,256]{1,0:T(8,128)(2,1)}, u32[]{:S(2)}, u32[]{:S(2)}) collective-permute-start(bf16[1984,256]{1,0:T(8,128)(2,1)} %get-tuple-element.34), channel_id=1, source_target_pairs={{0,2},{1,3},{2,0},{3,1},{4,6},{5,7},{6,4},{7,5},{8,10},{9,11},{10,... | collective-permute-start | bytes 3047432 | tf_op jit(solution)/shard_map/ppermute | solution.py:34
  114.0 4.6 %collective-permute-start.9 = (f32[8,4,7,4,128]{4,3,2,1,0:T(4,128)S(1)}, f32[8,4,7,4,128]{4,3,2,1,0:T(4,128)S(1)}, u32[]{:S(2)}, u32[]{:S(2)}) collective-permute-start(f32[8,4,7,4,128]{4,3,2,1,0:T(4,128)S(1)} %bitcast.7), channel_id=1, source_target_pairs={{0,4},{4,0},{1,5},{5,1},{2,6},{6,2},{3,7},{7,3},{8,12},{12,8},{9,1... | collective-permute-start | bytes 1376264 | tf_op jit(solution)/shard_map/ppermute | solution.py:34
  118.6 2.0 %copy-start = (f32[3584,256]{1,0:T(8,128)S(1)}, f32[3584,256]{1,0:T(8,128)}, u32[]{:S(2)}) copy-start(f32[3584,256]{1,0:T(8,128)} %get-tuple-element.30.merged_ref) | copy-start | bytes 11010052
  123.2 0.9 copy-start.3
  124.1 0.6 copy-start.7
  124.8 1.2 collective-permute-start.10
  126.7 8.1 %all-to-all-start.2 = ((f32[4,32,256]{2,1,0:T(8,128)}), f32[4,32,256]{2,1,0:T(8,128)S(1)}, u32[]{:S(2)}, u32[]{:S(2)}) async-start(f32[4,32,256]{2,1,0:T(8,128)} %broadcast_in_dim.6), calls=%async_computation.2 | async-start | bytes 262144 | tf_op jit(solution)/shard_map/all_to_all | solution.py:362
  134.8 10.7 %collective-permute-start.12 = (bf16[1984,256]{1,0:T(8,128)(2,1)}, bf16[1984,256]{1,0:T(8,128)(2,1)}, u32[]{:S(2)}, u32[]{:S(2)}) collective-permute-start(bf16[1984,256]{1,0:T(8,128)(2,1)} %collective-permute-done.7.refs_0_), channel_id=1, source_target_pairs={{0,4},{4,0},{1,5},{5,1},{2,6},{6,2},{3,7},{7,3},{8,12},{12,8},{9,1... | collective-permute-start | bytes 3047432 | tf_op jit(solution)/shard_map/ppermute | solution.py:34
  136.5 9.0 %collective-permute-start.13 = (bf16[1984,256]{1,0:T(8,128)(2,1)}, bf16[1984,256]{1,0:T(8,128)(2,1)}, u32[]{:S(2)}, u32[]{:S(2)}) collective-permute-start(bf16[1984,256]{1,0:T(8,128)(2,1)} %collective-permute-done.11.refs_1_), channel_id=1, source_target_pairs={{0,4},{4,0},{1,5},{5,1},{2,6},{6,2},{3,7},{7,3},{8,12},{12,8},{9,1... | collective-permute-start | bytes 3047432 | tf_op jit(solution)/shard_map/ppermute | solution.py:34
  136.6 8.9 %collective-permute-start.14 = (bf16[1984,256]{1,0:T(8,128)(2,1)}, bf16[1984,256]{1,0:T(8,128)(2,1)}, u32[]{:S(2)}, u32[]{:S(2)}) collective-permute-start(bf16[1984,256]{1,0:T(8,128)(2,1)} %collective-permute-done.8.refs_2_), channel_id=1, source_target_pairs={{0,4},{4,0},{1,5},{5,1},{2,6},{6,2},{3,7},{7,3},{8,12},{12,8},{9,1... | collective-permute-start | bytes 3047432 | tf_op jit(solution)/shard_map/ppermute | solution.py:34
  137.7 15.7 %all-to-all-start.3 = ((f32[8,32,256]{2,1,0:T(8,128)}), f32[8,32,256]{2,1,0:T(8,128)S(1)}, u32[]{:S(2)}, u32[]{:S(2)}) async-start(f32[8,32,256]{2,1,0:T(8,128)} %broadcast_in_dim.7), calls=%async_computation.3 | async-start | bytes 524288 | tf_op jit(solution)/shard_map/all_to_all | solution.py:370
  141.2 1.2 copy-start.4
  142.3 0.8 copy-start.5
  145.5 9.4 %copy-start.6 = (f32[64,64]{1,0:T(8,128)S(1)}, f32[64,64]{1,0:T(8,128)}, u32[]{:S(2)}) copy-start(f32[64,64]{1,0:T(8,128)} %inverse_factor.1.inverse_ref) | copy-start | bytes 49156
  153.5 1.4 collective-permute-start.15
  154.9 2.0 %copy-start.1 = (f32[3584,256]{1,0:T(8,128)S(1)}, f32[3584,256]{1,0:T(8,128)}, u32[]{:S(2)}) copy-start(f32[3584,256]{1,0:T(8,128)} %get-tuple-element.30.merged_ref) | copy-start | bytes 11010052

commit v3 on v2

--- a/solution.py
+++ b/solution.py
@@ -52,16 +52,33 @@
     return first[:rows] + (first[rows : 2 * rows] + second[:rows] + small)
 
 
-def merged_and_left(core, pieces, grads, error, right):
-    count = len(pieces)
-
-    def body(core_ref, *refs):
-        piece_refs = refs[:count]
-        grad_ref, error_ref, right_ref = refs[count : count + 3]
-        merged_ref, mine_ref, other_ref = refs[-3:]
+def started_merged(pieces, grads, error):
+    def body(*refs):
+        *piece_refs, grad_ref, error_ref, merged_ref = refs
         tokens = jnp.concatenate([ref[...] for ref in piece_refs], 0)
-        transposed = dot(grad_ref[...], tokens, 0, 0)
-        merged = transposed.T + error_ref[...].astype(F32)
+        near = jnp.concatenate([grad_ref[: 2 * PART], grad_ref[3 * PART :]], 0)
+        merged_ref[...] = dot(near, tokens, 0, 0).T + error_ref[...].astype(F32)
+
+    rows = pl.BlockSpec((STEP, COLUMNS), lambda i: (i, 0))
+    return pl.pallas_call(
+        body,
+        grid=(FEATURES // STEP,),
+        in_specs=[pl.BlockSpec((piece.shape[0], STEP), lambda i: (0, i)) for piece in pieces]
+        + [whole(grads), rows],
+        out_specs=rows,
+        out_shape=jax.ShapeDtypeStruct((FEATURES, COLUMNS), F32),
+        compiler_params=VMEM,
+        cost_estimate=SMALL,
+        name="started_merged",
+    )(*pieces, grads, error)
+
+
+def merged_and_left(core, far_low, far_high, grads, started, right):
+    def body(core_ref, low_ref, high_ref, grad_ref, started_ref, right_ref, *refs):
+        merged_ref, mine_ref, other_ref = refs
+        tokens = jnp.concatenate([low_ref[...], high_ref[...]], 0)
+        far = dot(grad_ref[2 * PART : 3 * PART], tokens, 0, 0)
+        merged = far.T + started_ref[...]
         merged_ref[...] = merged
         left = stacked_dot(right_ref[...], merged, 1)
         low, high = left[:HALF], left[HALF:]
@@ -73,23 +90,24 @@
                 mine_ref[row, 0, lane] = mine[tile]
                 other_ref[row, 0, lane] = other[tile]
 
+    rows = pl.BlockSpec((STEP, COLUMNS), lambda i: (i, 0))
+    columns = pl.BlockSpec((PART // 2, STEP), lambda i: (0, i))
     tiles = pl.BlockSpec((8, 1, 7, 4, 128), lambda i: (0, i, 0, 0, 0))
     return pl.pallas_call(
         body,
         grid=(FEATURES // STEP,),
-        in_specs=[pl.BlockSpec(memory_space=pltpu.SMEM)]
-        + [pl.BlockSpec((piece.shape[0], STEP), lambda i: (0, i)) for piece in pieces]
-        + [whole(grads), pl.BlockSpec((STEP, COLUMNS), lambda i: (i, 0)), whole(right)],
-        out_specs=[pl.BlockSpec((STEP, COLUMNS), lambda i: (i, 0)), tiles, tiles],
+        in_specs=[pl.BlockSpec(memory_space=pltpu.SMEM), columns, columns]
+        + [whole(grads), rows, whole(right)],
+        out_specs=[rows, tiles, tiles],
         out_shape=[
             jax.ShapeDtypeStruct((FEATURES, COLUMNS), F32),
             jax.ShapeDtypeStruct(TILES, F32),
             jax.ShapeDtypeStruct(TILES, F32),
         ],
-        compiler_params=ALL_VMEM,
+        compiler_params=VMEM,
         cost_estimate=SMALL,
         name="merged_and_left",
-    )(core, *pieces, grads, error, right)
+    )(core, far_low, far_high, grads, started, right)
 
 
 def ordered(core, mine, other):
@@ -334,13 +352,19 @@
     before_low, after_high = shift(low, "tensor", 4, 1), shift(high, "tensor", 4, -1)
     before_high, after_low = shift(high, "tensor", 4, 1), shift(low, "tensor", 4, -1)
     far_low, far_high = shift(before_low, "tensor", 4, 1), shift(after_high, "tensor", 4, -1)
-    pieces = (layer_input, after_low, after_high, far_low, far_high, before_low, before_high)
-    merged, mine, other = merged_and_left(core_word, pieces, grads, error, right_rows)
-
+    pieces = (layer_input, after_low, after_high, before_low, before_high)
     half = lax.dynamic_slice_in_dim(query_weight, core * HALF_FEATURES, HALF_FEATURES, 0)
     parcels = [
         jnp.concatenate([half, grads[k * PART : (k + 1) * PART]], 0) for k in (1, 2, 3)
     ]
+    ready_grads, parcels[0], parcels[2] = lax.optimization_barrier(
+        (grads, parcels[0], parcels[2])
+    )
+    started = started_merged(pieces, ready_grads, error)
+    merged, mine, other = merged_and_left(
+        core_word, far_low, far_high, grads, started, right_rows
+    )
+
     parcels = lax.optimization_barrier((*parcels, before_high))[:3]
     before, after = shift(parcels[0], "tensor", 4, 1), shift(parcels[2], "tensor", 4, -1)
 

time: 160 us -> 156 us (0.975)
  waiting for transfers between devices: 70.1 us -> 64.1 us
    ppermute x16, waiting for transfers between devices: 50.7 us -> 44.7 us  [shift(): lax.ppermute(value, axis, [(at, (at + by) % size) for at in range(size)])]
    pallas_call x0 -> x1, Pallas kernels: none -> 4.37 us  [started_merged(): pl.pallas_call(body, grid=(FEATURES // STEP,), in_specs=[pl.BlockSpec((pi...]
    pallas_call x1, Pallas kernels: 7.66 us -> 3.83 us  [merged_and_left(): pl.pallas_call(body, grid=(FEATURES // STEP,), in_specs=[pl.BlockSpec(mem...]
  transfers between devices with their start and end apart: 20 -> 20, of which waited for: 13 -> 13; matrix products, arithmetic and copies ran while one was open for 4% -> 4% of each run, Pallas kernels for 9% -> 12%
where the time goes in v3:
time: 156 us; the launch traced here: 155 us
  waiting for transfers between devices  64.1 us (41%)
  starting transfers between devices  47.8 us (31%)
  Pallas kernels  25.8 us (17%)
  local copies, waits for them, and re-layouts  12.8 us (8%)
  other arithmetic  4.04 us (3%)
    ppermute x16, waiting for transfers between devices, shift(): lax.ppermute(value, axis, [(at, (at + by) % size) for at in range(size)])  44.7 us
    ppermute x16, starting transfers between devices, shift(): lax.ppermute(value, axis, [(at, (at + by) % size) for at in range(size)])  22.8 us
    all_to_all x1, waiting for transfers between devices, shards(): mine = lax.all_to_all(copies, PLANE, 0, 0, tiled=True).reshape(TILES)  12 us
    all_to_all x1, starting transfers between devices, shards(): blocks = lax.all_to_all(total, PLANE, 0, 0, tiled=True)  11 us
    unnamed x22, local copies, waits for them, and re-layouts  8.73 us
    all_to_all x1, starting transfers between devices, shards(): mine = lax.all_to_all(copies, PLANE, 0, 0, tiled=True).reshape(TILES)  7.2 us
    pallas_call x1, Pallas kernels, input_gradient(): pl.pallas_call(body, grid_spec=pltpu.PrefetchScalarGridSpec(num_scalar_pr...  6.23 us
    pallas_call x1, Pallas kernels, started_merged(): pl.pallas_call(body, grid=(FEATURES // STEP,), in_specs=[pl.BlockSpec((pi...  4.37 us
  transfers between devices with their start and end apart: 20, of which 13 were waited for; matrix products, arithmetic and copies ran while one was open for 4% of the time, Pallas kernels for 12%

profile of v3, /device:TPU:1, one launch (start us, length us, event | category | flops | bytes accessed | tf_op | source)
XLA Modules:
  0.0 155.4 jit_solution(4285964044033413686)
XLA Ops:
  0.6 2.6 %fusion.1 = (bf16[96,3584]{1,0:T(8,128)(2,1)}, bf16[96,3584]{1,0:T(8,128)(2,1)}) fusion(bf16[192,3584]{1,0:T(8,128)(2,1)} %refs_0_.1), kind=kLoop, calls=%fused_computation.9 | loop fusion | bytes 2752512 | tf_op jit(solution)/shard_map/slice | solution.py:351
  3.3 2.1 %collective-permute-start = (bf16[96,3584]{1,0:T(8,128)(2,1)}, bf16[96,3584]{1,0:T(8,128)(2,1)S(1)}, u32[]{:S(2)}, u32[]{:S(2)}) collective-permute-start(bf16[96,3584]{1,0:T(8,128)(2,1)} %get-tuple-element.54), channel_id=1, source_target_pairs={{0,1},{1,2},{2,3},{3,0},{4,5},{5,6},{6,7},{7,4},{8,9},{9,10},{10,1... | collective-permute-start | bytes 2064392 | tf_op jit(solution)/shard_map/ppermute | solution.py:34
  5.4 1.4 collective-permute-start.2
  6.8 0.0 collective-permute-start.5
  6.9 2.7 %collective-permute-start.4 = (bf16[96,3584]{1,0:T(8,128)(2,1)}, bf16[96,3584]{1,0:T(8,128)(2,1)}, u32[]{:S(2)}, u32[]{:S(2)}) collective-permute-start(bf16[96,3584]{1,0:T(8,128)(2,1)} %get-tuple-element.54), channel_id=1, source_target_pairs={{0,3},{1,0},{2,1},{3,2},{4,7},{5,4},{6,5},{7,6},{8,11},{9,8},{10,9... | collective-permute-start | bytes 2064392 | tf_op jit(solution)/shard_map/ppermute | solution.py:34
  9.5 1.3 fusion.refs_5_.grad_ref
  10.8 9.4 %collective-permute-done.refs_3_ = bf16[96,3584]{1,0:T(8,128)(2,1)S(1)} collective-permute-done((bf16[96,3584]{1,0:T(8,128)(2,1)}, bf16[96,3584]{1,0:T(8,128)(2,1)S(1)}, u32[]{:S(2)}, u32[]{:S(2)}) %collective-permute-start) | collective-permute-done | bytes 688160 | tf_op jit(solution)/shard_map/ppermute | solution.py:34
  20.2 1.6 %collective-permute-start.1 = (bf16[96,3584]{1,0:T(8,128)(2,1)S(1)}, bf16[96,3584]{1,0:T(8,128)(2,1)S(1)}, u32[]{:S(2)}, u32[]{:S(2)}) collective-permute-start(bf16[96,3584]{1,0:T(8,128)(2,1)S(1)} %collective-permute-done.refs_3_), channel_id=1, source_target_pairs={{0,1},{1,2},{2,3},{3,0},{4,5},{5,6},{6,7},{7,4},{8,9},{9,10},{10,1... | collective-permute-start | bytes 2064392 | tf_op jit(solution)/shard_map/ppermute | solution.py:34
  21.7 0.0 collective-permute-done.2.refs_2_
  21.7 1.6 %collective-permute-start.3 = (bf16[96,3584]{1,0:T(8,128)(2,1)S(1)}, bf16[96,3584]{1,0:T(8,128)(2,1)S(1)}, u32[]{:S(2)}, u32[]{:S(2)}) collective-permute-start(bf16[96,3584]{1,0:T(8,128)(2,1)S(1)} %collective-permute-done.2.refs_2_), channel_id=1, source_target_pairs={{0,3},{1,0},{2,1},{3,2},{4,7},{5,4},{6,5},{7,6},{8,11},{9,8},{10,9... | collective-permute-start | bytes 2064392 | tf_op jit(solution)/shard_map/ppermute | solution.py:34
  23.4 0.1 constant_dynamic-slice_fusion.1
  23.5 0.0 copy-start.3
  23.5 0.0 copy-start.5
  23.5 1.8 %pad_maximum_fusion.2 = (bf16[1984,256]{1,0:T(8,128)(2,1)}, bf16[1984,256]{1,0:T(8,128)(2,1)}, bf16[1984,256]{1,0:T(8,128)(2,1)}) fusion(bf16[192,256]{1,0:T(8,128)(2,1)S(1)} %get-tuple-element.59, bf16[1792,256]{1,0:T(8,128)(2,1)S(1)} %constant_dynamic-slice_fusion.1, bf16[192,256]{1,0:T(8,128)(2,1)S(1)} %get-tuple-element.60, ...), kind=kLoop, calls=%fused_computation.2 | loop fusion | flops 5079040 | bytes 4259840 | tf_op jit(solution)/shard_map/concatenate | solution.py:358
  25.3 9.7 %collective-permute-done.5.refs_4_ = bf16[96,3584]{1,0:T(8,128)(2,1)} collective-permute-done((bf16[96,3584]{1,0:T(8,128)(2,1)}, bf16[96,3584]{1,0:T(8,128)(2,1)}, u32[]{:S(2)}, u32[]{:S(2)}) %collective-permute-start.5) | collective-permute-done | bytes 688160 | tf_op jit(solution)/shard_map/ppermute | solution.py:34
  35.0 1.3 collective-permute-done.4.refs_1_
  36.3 4.4 %started_merged.1.started_ref = f32[3584,256]{1,0:T(8,128)S(1)} custom-call(bf16[192,3584]{1,0:T(8,128)(2,1)S(1)} %copy-done.3, bf16[96,3584]{1,0:T(8,128)(2,1)} %collective-permute-done.4.refs_1_, bf16[96,3584]{1,0:T(8,128)(2,1)S(1)} %collective-permute-done.2.refs_2_, bf16[96,3584]{1,0:T(8,128)(2,1)S(1)} %collective-permute-done.refs_3_, ...), custom_call_target="tpu_custom_call" | custom-call | flops 1000 | bytes 1000 | tf_op jit(solution)/shard_map/started_merged/pallas_call | solution.py:63
  40.7 9.0 %collective-permute-done.1.low_ref = bf16[96,3584]{1,0:T(8,128)(2,1)S(1)} collective-permute-done((bf16[96,3584]{1,0:T(8,128)(2,1)S(1)}, bf16[96,3584]{1,0:T(8,128)(2,1)S(1)}, u32[]{:S(2)}, u32[]{:S(2)}) %collective-permute-start.1) | collective-permute-done | bytes 688160 | tf_op jit(solution)/shard_map/ppermute | solution.py:34
  49.7 1.3 collective-permute-done.3.high_ref
  50.9 3.8 %merged_and_left.1 = (f32[3584,256]{1,0:T(8,128)S(1)}, f32[8,4,7,4,128]{4,3,2,1,0:T(4,128)S(1)}, f32[8,4,7,4,128]{4,3,2,1,0:T(4,128)S(1)}) custom-call(s32[1]{0:T(128)} %bitcast.core_ref, bf16[96,3584]{1,0:T(8,128)(2,1)S(1)} %collective-permute-done.1.low_ref, bf16[96,3584]{1,0:T(8,128)(2,1)S(1)} %collective-permute-done.3.high_ref, ...), custom_call_target="tpu_custom_call" | custom-call | flops 1000 | bytes 1000 | tf_op jit(solution)/shard_map/merged_and_left/pallas_call | solution.py:96
  54.8 1.8 %copy-done = f32[3584,256]{1,0:T(8,128)} copy-done((f32[3584,256]{1,0:T(8,128)}, f32[3584,256]{1,0:T(8,128)S(1)}, u32[]{:S(2)}) %copy-start) | copy-done | bytes 3670040
  56.5 2.0 %collective-permute-start.6 = (f32[8,4,7,4,128]{4,3,2,1,0:T(4,128)S(1)}, f32[8,4,7,4,128]{4,3,2,1,0:T(4,128)S(1)}, u32[]{:S(2)}, u32[]{:S(2)}) collective-permute-start(f32[8,4,7,4,128]{4,3,2,1,0:T(4,128)S(1)} %get-tuple-element.30), channel_id=1, source_target_pairs={{0,4},{4,0},{1,5},{5,1},{2,6},{6,2},{3,7},{7,3},{8,12},{12,8},{9,1... | collective-permute-start | bytes 1376264 | tf_op jit(solution)/shard_map/ppermute | solution.py:34
  58.6 1.3 collective-permute-start.7
  59.9 1.4 collective-permute-start.8
  61.3 0.0 collective-permute-done.6
  61.3 0.9 add.20
  62.2 11.0 %all-to-all-start = ((f32[32,7,4,128]{3,2,1,0:T(4,128)}), f32[32,7,4,128]{3,2,1,0:T(4,128)S(1)}, u32[]{:S(2)}, u32[]{:S(2)}) async-start(f32[32,7,4,128]{3,2,1,0:T(4,128)} %bitcast.3), calls=%async_computation | async-start | bytes 917504 | tf_op jit(solution)/shard_map/all_to_all | solution.py:372
  73.2 11.0 %collective-permute-done.7.refs_0_ = bf16[1984,256]{1,0:T(8,128)(2,1)} collective-permute-done((bf16[1984,256]{1,0:T(8,128)(2,1)}, bf16[1984,256]{1,0:T(8,128)(2,1)}, u32[]{:S(2)}, u32[]{:S(2)}) %collective-permute-start.7) | collective-permute-done | bytes 1015840 | tf_op jit(solution)/shard_map/ppermute | solution.py:34
  84.2 0.0 collective-permute-done.8.refs_2_
  84.2 3.9 %all-to-all-done.blocks_ref = f32[32,7,4,128]{3,2,1,0:T(4,128)S(1)} async-done(((f32[32,7,4,128]{3,2,1,0:T(4,128)}), f32[32,7,4,128]{3,2,1,0:T(4,128)S(1)}, u32[]{:S(2)}, u32[]{:S(2)}) %all-to-all-start) | async-done | bytes 458784 | tf_op jit(solution)/shard_map/all_to_all | solution.py:372
  88.0 0.9 summed_copies.1
  88.9 7.2 %all-to-all-start.1 = ((f32[32,7,4,128]{3,2,1,0:T(4,128)}), f32[32,7,4,128]{3,2,1,0:T(4,128)S(1)}, u32[]{:S(2)}, u32[]{:S(2)}) async-start(f32[32,7,4,128]{3,2,1,0:T(4,128)} %summed_copies.1), calls=%async_computation.1 | async-start | bytes 917504 | tf_op jit(solution)/shard_map/all_to_all | solution.py:376
  96.1 2.4 %collective-permute-start.11 = (bf16[1984,256]{1,0:T(8,128)(2,1)}, bf16[1984,256]{1,0:T(8,128)(2,1)}, u32[]{:S(2)}, u32[]{:S(2)}) collective-permute-start(bf16[1984,256]{1,0:T(8,128)(2,1)} %get-tuple-element.40), channel_id=1, source_target_pairs={{0,2},{1,3},{2,0},{3,1},{4,6},{5,7},{6,4},{7,5},{8,10},{9,11},{10,... | collective-permute-start | bytes 3047432 | tf_op jit(solution)/shard_map/ppermute | solution.py:34
  98.5 12.0 %all-to-all-done.1 = f32[32,7,4,128]{3,2,1,0:T(4,128)S(1)} async-done(((f32[32,7,4,128]{3,2,1,0:T(4,128)}), f32[32,7,4,128]{3,2,1,0:T(4,128)S(1)}, u32[]{:S(2)}, u32[]{:S(2)}) %all-to-all-start.1) | async-done | bytes 458784 | tf_op jit(solution)/shard_map/all_to_all | solution.py:376
  110.5 3.2 %collective-permute-start.9 = (f32[8,4,7,4,128]{4,3,2,1,0:T(4,128)S(1)}, f32[8,4,7,4,128]{4,3,2,1,0:T(4,128)S(1)}, u32[]{:S(2)}, u32[]{:S(2)}) collective-permute-start(f32[8,4,7,4,128]{4,3,2,1,0:T(4,128)S(1)} %bitcast.7), channel_id=1, source_target_pairs={{0,4},{4,0},{1,5},{5,1},{2,6},{6,2},{3,7},{7,3},{8,12},{12,8},{9,1... | collective-permute-start | bytes 1376264 | tf_op jit(solution)/shard_map/ppermute | solution.py:34
  113.7 1.4 collective-permute-done.9.other_ref
  115.1 2.0 %copy-done.1 = f32[3584,256]{1,0:T(8,128)S(1)} copy-done((f32[3584,256]{1,0:T(8,128)S(1)}, f32[3584,256]{1,0:T(8,128)}, u32[]{:S(2)}) %copy-start.1) | copy-done | bytes 3670040
  117.2 2.6 %cross_and_gram.1 = (f32[64,3584]{1,0:T(8,128)S(1)}, f32[64,256]{1,0:T(8,128)S(1)}, f32[64,64]{1,0:T(8,128)S(1)}) custom-call(s32[1]{0:T(128)} %bitcast.core_ref, f32[8,4,7,4,128]{4,3,2,1,0:T(4,128)S(1)} %bitcast.8, f32[8,4,7,4,128]{4,3,2,1,0:T(4,128)S(1)} %collective-permute-done.9.other_ref, f32[3584,256]{1,0:T(8,128)S(1)} %copy-done.1), custom_call_target="tpu_custom_call" | custom-call | flops 1000 | bytes 1000 | tf_op jit(solution)/shard_map/cross_and_gram/pallas_call | solution.py:144
  119.7 0.0 copy-start.6
  119.7 0.9 copy-done.6
  120.6 0.4 collective-permute-start.10
  121.0 0.9 collective-permute-done.10
  121.9 0.7 broadcast_in_dim.6
  122.5 3.3 %all-to-all-start.2 = ((f32[4,32,256]{2,1,0:T(8,128)}), f32[4,32,256]{2,1,0:T(8,128)S(1)}, u32[]{:S(2)}, u32[]{:S(2)}) async-start(f32[4,32,256]{2,1,0:T(8,128)} %broadcast_in_dim.6), calls=%async_computation.2 | async-start | bytes 262144 | tf_op jit(solution)/shard_map/all_to_all | solution.py:386
  125.9 3.0 %inverse_factor.1.inverse_ref = f32[64,64]{1,0:T(8,128)} custom-call(f32[64,64]{1,0:T(8,128)} %copy-done.10), custom_call_target="tpu_custom_call" | custom-call | flops 1000 | bytes 1000 | tf_op jit(solution)/shard_map/inverse_factor/pallas_call | solution.py:207
  128.9 1.8 %all-to-all-done.2 = f32[4,32,256]{2,1,0:T(8,128)S(1)} async-done(((f32[4,32,256]{2,1,0:T(8,128)}), f32[4,32,256]{2,1,0:T(8,128)S(1)}, u32[]{:S(2)}, u32[]{:S(2)}) %all-to-all-start.2) | async-done | bytes 131104 | tf_op jit(solution)/shard_map/all_to_all | solution.py:386
  130.7 0.0 collective-permute-done.11.refs_1_
  130.7 1.7 %collective-permute-start.12 = (bf16[1984,256]{1,0:T(8,128)(2,1)}, bf16[1984,256]{1,0:T(8,128)(2,1)}, u32[]{:S(2)}, u32[]{:S(2)}) collective-permute-start(bf16[1984,256]{1,0:T(8,128)(2,1)} %collective-permute-done.7.refs_0_), channel_id=1, source_target_pairs={{0,4},{4,0},{1,5},{5,1},{2,6},{6,2},{3,7},{7,3},{8,12},{12,8},{9,1... | collective-permute-start | bytes 3047432 | tf_op jit(solution)/shard_map/ppermute | solution.py:34
  132.4 0.1 collective-permute-start.13
  132.5 0.4 collective-permute-start.14
  132.9 0.7 broadcast_in_dim.7
  133.6 3.4 %all-to-all-start.3 = ((f32[8,32,256]{2,1,0:T(8,128)}), f32[8,32,256]{2,1,0:T(8,128)S(1)}, u32[]{:S(2)}, u32[]{:S(2)}) async-start(f32[8,32,256]{2,1,0:T(8,128)} %broadcast_in_dim.7), calls=%async_computation.3 | async-start | bytes 524288 | tf_op jit(solution)/shard_map/all_to_all | solution.py:394
  137.0 0.0 copy-start.7
  137.1 1.2 copy-done.7
  138.2 0.8 copy-done.8
  139.0 2.4 %orthonormal.1.basis_ref = bf16[3584,128]{1,0:T(8,128)(2,1)S(1)} custom-call(f32[64,64]{1,0:T(8,128)S(1)} %copy-done.8, f32[64,3584]{1,0:T(8,128)S(1)} %copy-done.7), custom_call_target="tpu_custom_call" | custom-call | flops 1000 | bytes 1000 | tf_op jit(solution)/shard_map/orthonormal/pallas_call | solution.py:222
  141.4 0.0 collective-permute-done.13.refs_4_
  141.4 0.0 collective-permute-done.14.refs_5_
  141.4 6.2 %input_gradient.1 = bf16[192,3584]{1,0:T(8,128)(2,1)} custom-call(s32[1]{0:T(128)} %bitcast.core_ref, bf16[192,256]{1,0:T(8,128)(2,1)S(1)} %get-tuple-element.58.grad_ref, bf16[3584,256]{1,0:T(8,128)(2,1)S(1)} %copy-done.4, bf16[1984,256]{1,0:T(8,128)(2,1)} %collective-permute-done.7.refs_0_, bf16[1984,256]{1,0:T(8,128)(2,1)} %collective-permute-done.11.refs_1_, ...), custom_call_target="tpu_custom_call" | custom-call | flops 1000 | bytes 1000 | tf_op jit(solution)/shard_map/input_gradient/pallas_call | solution.py:299
  147.6 1.7 %all-to-all-done.3 = f32[8,32,256]{2,1,0:T(8,128)S(1)} async-done(((f32[8,32,256]{2,1,0:T(8,128)}), f32[8,32,256]{2,1,0:T(8,128)S(1)}, u32[]{:S(2)}, u32[]{:S(2)}) %all-to-all-start.3) | async-done | bytes 262176 | tf_op jit(solution)/shard_map/all_to_all | solution.py:394
  149.4 0.5 collective-permute-start.15
  149.9 0.9 collective-permute-done.15.other_ref
  150.8 2.0 %copy-done.2 = f32[3584,256]{1,0:T(8,128)S(1)} copy-done((f32[3584,256]{1,0:T(8,128)S(1)}, f32[3584,256]{1,0:T(8,128)}, u32[]{:S(2)}) %copy-start.2) | copy-done | bytes 3670040
  152.8 2.6 %finish.1 = (bf16[3584,256]{1,0:T(8,128)(2,1)}, f32[64,256]{1,0:T(8,128)}) custom-call(s32[1]{0:T(128)} %bitcast.core_ref, f32[32,256]{1,0:T(8,128)S(1)} %reduce_sum.19.mine_ref, f32[32,256]{1,0:T(8,128)S(1)} %collective-permute-done.15.other_ref, f32[64,64]{1,0:T(8,128)S(1)} %copy-done.8, bf16[3584,128]{1,0:T(8,128)(2,1)S(1)} %orthonormal.1.basis_ref, ...), custom_call_target="tpu_custom_call" | custom-call | flops 1000 | bytes 1000 | tf_op jit(solution)/shard_map/finish/pallas_call | solution.py:252
  (18 shorter events, 0.1 us)
Async XLA Ops:
  0.6 22.8 %copy-start.4 = (bf16[3584,256]{1,0:T(8,128)(2,1)S(1)}, bf16[3584,256]{1,0:T(8,128)(2,1)}, u32[]{:S(2)}) copy-start(bf16[3584,256]{1,0:T(8,128)(2,1)} %weight_ref.1) | copy-start | bytes 5505028
  3.3 16.9 %collective-permute-start = (bf16[96,3584]{1,0:T(8,128)(2,1)}, bf16[96,3584]{1,0:T(8,128)(2,1)S(1)}, u32[]{:S(2)}, u32[]{:S(2)}) collective-permute-start(bf16[96,3584]{1,0:T(8,128)(2,1)} %get-tuple-element.54), channel_id=1, source_target_pairs={{0,1},{1,2},{2,3},{3,0},{4,5},{5,6},{6,7},{7,4},{8,9},{9,10},{10,1... | collective-permute-start | bytes 2064392 | tf_op jit(solution)/shard_map/ppermute | solution.py:34
  5.4 16.3 %collective-permute-start.2 = (bf16[96,3584]{1,0:T(8,128)(2,1)}, bf16[96,3584]{1,0:T(8,128)(2,1)S(1)}, u32[]{:S(2)}, u32[]{:S(2)}) collective-permute-start(bf16[96,3584]{1,0:T(8,128)(2,1)} %get-tuple-element.53), channel_id=1, source_target_pairs={{0,3},{1,0},{2,1},{3,2},{4,7},{5,4},{6,5},{7,6},{8,11},{9,8},{10,9... | collective-permute-start | bytes 2064392 | tf_op jit(solution)/shard_map/ppermute | solution.py:34
  6.8 28.2 %collective-permute-start.5 = (bf16[96,3584]{1,0:T(8,128)(2,1)}, bf16[96,3584]{1,0:T(8,128)(2,1)}, u32[]{:S(2)}, u32[]{:S(2)}) collective-permute-start(bf16[96,3584]{1,0:T(8,128)(2,1)} %get-tuple-element.53), channel_id=1, source_target_pairs={{0,1},{1,2},{2,3},{3,0},{4,5},{5,6},{6,7},{7,4},{8,9},{9,10},{10,1... | collective-permute-start | bytes 2064392 | tf_op jit(solution)/shard_map/ppermute | solution.py:34
  6.9 29.4 %collective-permute-start.4 = (bf16[96,3584]{1,0:T(8,128)(2,1)}, bf16[96,3584]{1,0:T(8,128)(2,1)}, u32[]{:S(2)}, u32[]{:S(2)}) collective-permute-start(bf16[96,3584]{1,0:T(8,128)(2,1)} %get-tuple-element.54), channel_id=1, source_target_pairs={{0,3},{1,0},{2,1},{3,2},{4,7},{5,4},{6,5},{7,6},{8,11},{9,8},{10,9... | collective-permute-start | bytes 2064392 | tf_op jit(solution)/shard_map/ppermute | solution.py:34
  20.2 29.5 %collective-permute-start.1 = (bf16[96,3584]{1,0:T(8,128)(2,1)S(1)}, bf16[96,3584]{1,0:T(8,128)(2,1)S(1)}, u32[]{:S(2)}, u32[]{:S(2)}) collective-permute-start(bf16[96,3584]{1,0:T(8,128)(2,1)S(1)} %collective-permute-done.refs_3_), channel_id=1, source_target_pairs={{0,1},{1,2},{2,3},{3,0},{4,5},{5,6},{6,7},{7,4},{8,9},{9,10},{10,1... | collective-permute-start | bytes 2064392 | tf_op jit(solution)/shard_map/ppermute | solution.py:34
  21.7 29.2 %collective-permute-start.3 = (bf16[96,3584]{1,0:T(8,128)(2,1)S(1)}, bf16[96,3584]{1,0:T(8,128)(2,1)S(1)}, u32[]{:S(2)}, u32[]{:S(2)}) collective-permute-start(bf16[96,3584]{1,0:T(8,128)(2,1)S(1)} %collective-permute-done.2.refs_2_), channel_id=1, source_target_pairs={{0,3},{1,0},{2,1},{3,2},{4,7},{5,4},{6,5},{7,6},{8,11},{9,8},{10,9... | collective-permute-start | bytes 2064392 | tf_op jit(solution)/shard_map/ppermute | solution.py:34
  23.5 12.8 %copy-start.3 = (bf16[192,3584]{1,0:T(8,128)(2,1)S(1)}, bf16[192,3584]{1,0:T(8,128)(2,1)}, u32[]{:S(2)}) copy-start(bf16[192,3584]{1,0:T(8,128)(2,1)} %refs_0_.1) | copy-start | bytes 4128772
  23.5 12.8 %copy-start.5 = (bf16[1,3584,256]{2,1,0:T(8,128)(2,1)S(1)}, bf16[1,3584,256]{2,1,0:T(8,128)(2,1)}, u32[]{:S(2)}) copy-start(bf16[1,3584,256]{2,1,0:T(8,128)(2,1)} %param.8) | copy-start | bytes 5505028
  36.3 14.6 %copy-start.9 = (f32[256,64]{0,1:T(8,128)S(1)}, f32[256,64]{0,1:T(8,128)}, u32[]{:S(2)}) copy-start(f32[256,64]{0,1:T(8,128)} %param.9) | copy-start | bytes 196612
  54.8 1.8 %copy-start = (f32[3584,256]{1,0:T(8,128)}, f32[3584,256]{1,0:T(8,128)S(1)}, u32[]{:S(2)}) copy-start(f32[3584,256]{1,0:T(8,128)S(1)} %get-tuple-element.36.merged_ref) | copy-start | bytes 11010052
  56.5 4.7 %collective-permute-start.6 = (f32[8,4,7,4,128]{4,3,2,1,0:T(4,128)S(1)}, f32[8,4,7,4,128]{4,3,2,1,0:T(4,128)S(1)}, u32[]{:S(2)}, u32[]{:S(2)}) collective-permute-start(f32[8,4,7,4,128]{4,3,2,1,0:T(4,128)S(1)} %get-tuple-element.30), channel_id=1, source_target_pairs={{0,4},{4,0},{1,5},{5,1},{2,6},{6,2},{3,7},{7,3},{8,12},{12,8},{9,1... | collective-permute-start | bytes 1376264 | tf_op jit(solution)/shard_map/ppermute | solution.py:34
  58.6 25.6 %collective-permute-start.7 = (bf16[1984,256]{1,0:T(8,128)(2,1)}, bf16[1984,256]{1,0:T(8,128)(2,1)}, u32[]{:S(2)}, u32[]{:S(2)}) collective-permute-start(bf16[1984,256]{1,0:T(8,128)(2,1)} %get-tuple-element.33), channel_id=1, source_target_pairs={{0,1},{1,2},{2,3},{3,0},{4,5},{5,6},{6,7},{7,4},{8,9},{9,10},{10,1... | collective-permute-start | bytes 3047432 | tf_op jit(solution)/shard_map/ppermute | solution.py:34
  59.9 24.3 %collective-permute-start.8 = (bf16[1984,256]{1,0:T(8,128)(2,1)}, bf16[1984,256]{1,0:T(8,128)(2,1)}, u32[]{:S(2)}, u32[]{:S(2)}) collective-permute-start(bf16[1984,256]{1,0:T(8,128)(2,1)} %get-tuple-element.34), channel_id=1, source_target_pairs={{0,3},{1,0},{2,1},{3,2},{4,7},{5,4},{6,5},{7,6},{8,11},{9,8},{10,9... | collective-permute-start | bytes 3047432 | tf_op jit(solution)/shard_map/ppermute | solution.py:34
  62.2 25.9 %all-to-all-start = ((f32[32,7,4,128]{3,2,1,0:T(4,128)}), f32[32,7,4,128]{3,2,1,0:T(4,128)S(1)}, u32[]{:S(2)}, u32[]{:S(2)}) async-start(f32[32,7,4,128]{3,2,1,0:T(4,128)} %bitcast.3), calls=%async_computation | async-start | bytes 917504 | tf_op jit(solution)/shard_map/all_to_all | solution.py:372
  88.9 21.6 %all-to-all-start.1 = ((f32[32,7,4,128]{3,2,1,0:T(4,128)}), f32[32,7,4,128]{3,2,1,0:T(4,128)S(1)}, u32[]{:S(2)}, u32[]{:S(2)}) async-start(f32[32,7,4,128]{3,2,1,0:T(4,128)} %summed_copies.1), calls=%async_computation.1 | async-start | bytes 917504 | tf_op jit(solution)/shard_map/all_to_all | solution.py:376
  96.1 34.6 %collective-permute-start.11 = (bf16[1984,256]{1,0:T(8,128)(2,1)}, bf16[1984,256]{1,0:T(8,128)(2,1)}, u32[]{:S(2)}, u32[]{:S(2)}) collective-permute-start(bf16[1984,256]{1,0:T(8,128)(2,1)} %get-tuple-element.40), channel_id=1, source_target_pairs={{0,2},{1,3},{2,0},{3,1},{4,6},{5,7},{6,4},{7,5},{8,10},{9,11},{10,... | collective-permute-start | bytes 3047432 | tf_op jit(solution)/shard_map/ppermute | solution.py:34
  110.5 4.6 %collective-permute-start.9 = (f32[8,4,7,4,128]{4,3,2,1,0:T(4,128)S(1)}, f32[8,4,7,4,128]{4,3,2,1,0:T(4,128)S(1)}, u32[]{:S(2)}, u32[]{:S(2)}) collective-permute-start(f32[8,4,7,4,128]{4,3,2,1,0:T(4,128)S(1)} %bitcast.7), channel_id=1, source_target_pairs={{0,4},{4,0},{1,5},{5,1},{2,6},{6,2},{3,7},{7,3},{8,12},{12,8},{9,1... | collective-permute-start | bytes 1376264 | tf_op jit(solution)/shard_map/ppermute | solution.py:34
  115.1 2.0 %copy-start.1 = (f32[3584,256]{1,0:T(8,128)S(1)}, f32[3584,256]{1,0:T(8,128)}, u32[]{:S(2)}) copy-start(f32[3584,256]{1,0:T(8,128)} %copy-done) | copy-start | bytes 11010052
  119.7 0.9 copy-start.6
  120.6 5.2 %copy-start.10 = (f32[64,64]{1,0:T(8,128)}, f32[64,64]{1,0:T(8,128)S(1)}, u32[]{:S(2)}) copy-start(f32[64,64]{1,0:T(8,128)S(1)} %get-tuple-element.38.gram_ref) | copy-start | bytes 49156
  120.6 1.2 collective-permute-start.10
  122.5 8.1 %all-to-all-start.2 = ((f32[4,32,256]{2,1,0:T(8,128)}), f32[4,32,256]{2,1,0:T(8,128)S(1)}, u32[]{:S(2)}, u32[]{:S(2)}) async-start(f32[4,32,256]{2,1,0:T(8,128)} %broadcast_in_dim.6), calls=%async_computation.2 | async-start | bytes 262144 | tf_op jit(solution)/shard_map/all_to_all | solution.py:386
  130.7 10.7 %collective-permute-start.12 = (bf16[1984,256]{1,0:T(8,128)(2,1)}, bf16[1984,256]{1,0:T(8,128)(2,1)}, u32[]{:S(2)}, u32[]{:S(2)}) collective-permute-start(bf16[1984,256]{1,0:T(8,128)(2,1)} %collective-permute-done.7.refs_0_), channel_id=1, source_target_pairs={{0,4},{4,0},{1,5},{5,1},{2,6},{6,2},{3,7},{7,3},{8,12},{12,8},{9,1... | collective-permute-start | bytes 3047432 | tf_op jit(solution)/shard_map/ppermute | solution.py:34
  132.4 9.0 %collective-permute-start.13 = (bf16[1984,256]{1,0:T(8,128)(2,1)}, bf16[1984,256]{1,0:T(8,128)(2,1)}, u32[]{:S(2)}, u32[]{:S(2)}) collective-permute-start(bf16[1984,256]{1,0:T(8,128)(2,1)} %collective-permute-done.11.refs_1_), channel_id=1, source_target_pairs={{0,4},{4,0},{1,5},{5,1},{2,6},{6,2},{3,7},{7,3},{8,12},{12,8},{9,1... | collective-permute-start | bytes 3047432 | tf_op jit(solution)/shard_map/ppermute | solution.py:34
  132.5 8.9 %collective-permute-start.14 = (bf16[1984,256]{1,0:T(8,128)(2,1)}, bf16[1984,256]{1,0:T(8,128)(2,1)}, u32[]{:S(2)}, u32[]{:S(2)}) collective-permute-start(bf16[1984,256]{1,0:T(8,128)(2,1)} %collective-permute-done.8.refs_2_), channel_id=1, source_target_pairs={{0,4},{4,0},{1,5},{5,1},{2,6},{6,2},{3,7},{7,3},{8,12},{12,8},{9,1... | collective-permute-start | bytes 3047432 | tf_op jit(solution)/shard_map/ppermute | solution.py:34
  133.6 15.7 %all-to-all-start.3 = ((f32[8,32,256]{2,1,0:T(8,128)}), f32[8,32,256]{2,1,0:T(8,128)S(1)}, u32[]{:S(2)}, u32[]{:S(2)}) async-start(f32[8,32,256]{2,1,0:T(8,128)} %broadcast_in_dim.7), calls=%async_computation.3 | async-start | bytes 524288 | tf_op jit(solution)/shard_map/all_to_all | solution.py:394
  137.0 1.2 copy-start.7
  138.2 0.8 copy-start.8
  149.4 1.4 collective-permute-start.15
  150.8 2.0 %copy-start.2 = (f32[3584,256]{1,0:T(8,128)S(1)}, f32[3584,256]{1,0:T(8,128)}, u32[]{:S(2)}) copy-start(f32[3584,256]{1,0:T(8,128)} %copy-done) | copy-start | bytes 11010052

commit v4 on v3

--- a/solution.py
+++ b/solution.py
@@ -333,6 +333,32 @@
     )(blocks)
 
 
+def row_halves(array):
+    half = array.shape[0] // 2
+
+    def body(array_ref, low_ref, high_ref, semaphores):
+        copies = [
+            pltpu.make_async_copy(array_ref.at[pl.ds(0, half)], low_ref, semaphores.at[0]),
+            pltpu.make_async_copy(array_ref.at[pl.ds(half, half)], high_ref, semaphores.at[1]),
+        ]
+        for copy in copies:
+            copy.start()
+        for copy in copies:
+            copy.wait()
+
+    shape = jax.ShapeDtypeStruct((half, array.shape[1]), array.dtype)
+    return pl.pallas_call(
+        body,
+        in_specs=[pl.BlockSpec(memory_space=pl.ANY)],
+        out_specs=[pl.BlockSpec(memory_space=pl.ANY)] * 2,
+        out_shape=[shape, shape],
+        scratch_shapes=[pltpu.SemaphoreType.DMA((2,))],
+        compiler_params=VMEM,
+        cost_estimate=SMALL,
+        name="row_halves",
+    )(array)
+
+
 def both_ways(value):
     return shift(value, "tensor", 4, 1), shift(value, "tensor", 4, -1)
 
@@ -348,7 +374,7 @@
     )
     right_rows = right_prev.T
 
-    low, high = layer_input[: PART // 2], layer_input[PART // 2 :]
+    low, high = row_halves(layer_input)
     before_low, after_high = shift(low, "tensor", 4, 1), shift(high, "tensor", 4, -1)
     before_high, after_low = shift(high, "tensor", 4, 1), shift(low, "tensor", 4, -1)
     far_low, far_high = shift(before_low, "tensor", 4, 1), shift(after_high, "tensor", 4, -1)

time: 156 us -> 156 us (level)
    slice x1 -> x0, local copies, waits for them, and re-layouts: 2.63 us -> none  [shards(): low, high = (layer_input[:PART // 2], layer_input[PART // 2:])]
    unnamed x22 -> x24, local copies, waits for them, and re-layouts: 8.73 us -> 10.1 us
where the time goes in v4:
time: 156 us; the launch traced here: 155 us
  waiting for transfers between devices  64.2 us (41%)
  starting transfers between devices  47.8 us (31%)
  Pallas kernels  27 us (17%)
  local copies, waits for them, and re-layouts  11.6 us (7%)
  other arithmetic  4.03 us (3%)
    ppermute x16, waiting for transfers between devices, shift(): lax.ppermute(value, axis, [(at, (at + by) % size) for at in range(size)])  44.7 us
    ppermute x16, starting transfers between devices, shift(): lax.ppermute(value, axis, [(at, (at + by) % size) for at in range(size)])  23 us
    all_to_all x1, waiting for transfers between devices, shards(): mine = lax.all_to_all(copies, PLANE, 0, 0, tiled=True).reshape(TILES)  12.1 us
    all_to_all x1, starting transfers between devices, shards(): blocks = lax.all_to_all(total, PLANE, 0, 0, tiled=True)  11 us
    unnamed x24, local copies, waits for them, and re-layouts  10.1 us
    all_to_all x1, starting transfers between devices, shards(): mine = lax.all_to_all(copies, PLANE, 0, 0, tiled=True).reshape(TILES)  7.02 us
    pallas_call x1, Pallas kernels, input_gradient(): pl.pallas_call(body, grid_spec=pltpu.PrefetchScalarGridSpec(num_scalar_pr...  6.23 us
    pallas_call x1, Pallas kernels, started_merged(): pl.pallas_call(body, grid=(FEATURES // STEP,), in_specs=[pl.BlockSpec((pi...  4.37 us
  transfers between devices with their start and end apart: 20, of which 13 were waited for; matrix products, arithmetic and copies ran while one was open for 4% of the time, Pallas kernels for 12%

profile of v4, /device:TPU:1, one launch (start us, length us, event | category | flops | bytes accessed | tf_op | source)
XLA Modules:
  0.0 155.5 jit_solution(4030987413978459096)
XLA Ops:
  0.6 0.0 copy-start.3
  0.6 1.3 copy-done.3
  2.0 1.1 row_halves.1
  3.1 2.2 %collective-permute-start = (bf16[96,3584]{1,0:T(8,128)(2,1)}, bf16[96,3584]{1,0:T(8,128)(2,1)S(1)}, u32[]{:S(2)}, u32[]{:S(2)}) collective-permute-start(bf16[96,3584]{1,0:T(8,128)(2,1)} %get-tuple-element.30), channel_id=1, source_target_pairs={{0,1},{1,2},{2,3},{3,0},{4,5},{5,6},{6,7},{7,4},{8,9},{9,10},{10,1... | collective-permute-start | bytes 2064392 | tf_op jit(solution)/shard_map/ppermute | solution.py:34
  5.3 1.5 collective-permute-start.2
  6.8 0.0 collective-permute-start.5
  6.8 2.7 %collective-permute-start.4 = (bf16[96,3584]{1,0:T(8,128)(2,1)}, bf16[96,3584]{1,0:T(8,128)(2,1)}, u32[]{:S(2)}, u32[]{:S(2)}) collective-permute-start(bf16[96,3584]{1,0:T(8,128)(2,1)} %get-tuple-element.30), channel_id=1, source_target_pairs={{0,3},{1,0},{2,1},{3,2},{4,7},{5,4},{6,5},{7,6},{8,11},{9,8},{10,9... | collective-permute-start | bytes 2064392 | tf_op jit(solution)/shard_map/ppermute | solution.py:34
  9.5 1.3 fusion.refs_5_.grad_ref
  10.8 9.3 %collective-permute-done.refs_3_ = bf16[96,3584]{1,0:T(8,128)(2,1)S(1)} collective-permute-done((bf16[96,3584]{1,0:T(8,128)(2,1)}, bf16[96,3584]{1,0:T(8,128)(2,1)S(1)}, u32[]{:S(2)}, u32[]{:S(2)}) %collective-permute-start) | collective-permute-done | bytes 688160 | tf_op jit(solution)/shard_map/ppermute | solution.py:34
  20.1 1.6 %collective-permute-start.1 = (bf16[96,3584]{1,0:T(8,128)(2,1)S(1)}, bf16[96,3584]{1,0:T(8,128)(2,1)S(1)}, u32[]{:S(2)}, u32[]{:S(2)}) collective-permute-start(bf16[96,3584]{1,0:T(8,128)(2,1)S(1)} %collective-permute-done.refs_3_), channel_id=1, source_target_pairs={{0,1},{1,2},{2,3},{3,0},{4,5},{5,6},{6,7},{7,4},{8,9},{9,10},{10,1... | collective-permute-start | bytes 2064392 | tf_op jit(solution)/shard_map/ppermute | solution.py:34
  21.6 0.0 collective-permute-done.2.refs_2_
  21.6 1.6 %collective-permute-start.3 = (bf16[96,3584]{1,0:T(8,128)(2,1)S(1)}, bf16[96,3584]{1,0:T(8,128)(2,1)S(1)}, u32[]{:S(2)}, u32[]{:S(2)}) collective-permute-start(bf16[96,3584]{1,0:T(8,128)(2,1)S(1)} %collective-permute-done.2.refs_2_), channel_id=1, source_target_pairs={{0,3},{1,0},{2,1},{3,2},{4,7},{5,4},{6,5},{7,6},{8,11},{9,8},{10,9... | collective-permute-start | bytes 2064392 | tf_op jit(solution)/shard_map/ppermute | solution.py:34
  23.3 0.1 constant_dynamic-slice_fusion.1
  23.4 0.0 copy-start.4
  23.4 0.0 copy-start.6
  23.4 1.8 %pad_maximum_fusion.2 = (bf16[1984,256]{1,0:T(8,128)(2,1)}, bf16[1984,256]{1,0:T(8,128)(2,1)}, bf16[1984,256]{1,0:T(8,128)(2,1)}) fusion(bf16[192,256]{1,0:T(8,128)(2,1)S(1)} %get-tuple-element.61, bf16[1792,256]{1,0:T(8,128)(2,1)S(1)} %constant_dynamic-slice_fusion.1, bf16[192,256]{1,0:T(8,128)(2,1)S(1)} %get-tuple-element.62, ...), kind=kLoop, calls=%fused_computation.2 | loop fusion | flops 5079040 | bytes 4259840 | tf_op jit(solution)/shard_map/concatenate | solution.py:384
  25.2 9.7 %collective-permute-done.5.refs_4_ = bf16[96,3584]{1,0:T(8,128)(2,1)} collective-permute-done((bf16[96,3584]{1,0:T(8,128)(2,1)}, bf16[96,3584]{1,0:T(8,128)(2,1)}, u32[]{:S(2)}, u32[]{:S(2)}) %collective-permute-start.5) | collective-permute-done | bytes 688160 | tf_op jit(solution)/shard_map/ppermute | solution.py:34
  34.9 1.2 collective-permute-done.4.refs_1_
  36.1 4.4 %started_merged.1.started_ref = f32[3584,256]{1,0:T(8,128)S(1)} custom-call(bf16[192,3584]{1,0:T(8,128)(2,1)S(1)} %copy-done.4, bf16[96,3584]{1,0:T(8,128)(2,1)} %collective-permute-done.4.refs_1_, bf16[96,3584]{1,0:T(8,128)(2,1)S(1)} %collective-permute-done.2.refs_2_, bf16[96,3584]{1,0:T(8,128)(2,1)S(1)} %collective-permute-done.refs_3_, ...), custom_call_target="tpu_custom_call" | custom-call | flops 1000 | bytes 1000 | tf_op jit(solution)/shard_map/started_merged/pallas_call | solution.py:63
  40.5 9.1 %collective-permute-done.1.low_ref = bf16[96,3584]{1,0:T(8,128)(2,1)S(1)} collective-permute-done((bf16[96,3584]{1,0:T(8,128)(2,1)S(1)}, bf16[96,3584]{1,0:T(8,128)(2,1)S(1)}, u32[]{:S(2)}, u32[]{:S(2)}) %collective-permute-start.1) | collective-permute-done | bytes 688160 | tf_op jit(solution)/shard_map/ppermute | solution.py:34
  49.6 1.2 collective-permute-done.3.high_ref
  50.7 3.8 %merged_and_left.1 = (f32[3584,256]{1,0:T(8,128)S(1)}, f32[8,4,7,4,128]{4,3,2,1,0:T(4,128)S(1)}, f32[8,4,7,4,128]{4,3,2,1,0:T(4,128)S(1)}) custom-call(s32[1]{0:T(128)} %bitcast.core_ref, bf16[96,3584]{1,0:T(8,128)(2,1)S(1)} %collective-permute-done.1.low_ref, bf16[96,3584]{1,0:T(8,128)(2,1)S(1)} %collective-permute-done.3.high_ref, ...), custom_call_target="tpu_custom_call" | custom-call | flops 1000 | bytes 1000 | tf_op jit(solution)/shard_map/merged_and_left/pallas_call | solution.py:96
  54.6 1.8 %copy-done = f32[3584,256]{1,0:T(8,128)} copy-done((f32[3584,256]{1,0:T(8,128)}, f32[3584,256]{1,0:T(8,128)S(1)}, u32[]{:S(2)}) %copy-start) | copy-done | bytes 3670040
  56.4 2.1 %collective-permute-start.6 = (f32[8,4,7,4,128]{4,3,2,1,0:T(4,128)S(1)}, f32[8,4,7,4,128]{4,3,2,1,0:T(4,128)S(1)}, u32[]{:S(2)}, u32[]{:S(2)}) collective-permute-start(f32[8,4,7,4,128]{4,3,2,1,0:T(4,128)S(1)} %get-tuple-element.34), channel_id=1, source_target_pairs={{0,4},{4,0},{1,5},{5,1},{2,6},{6,2},{3,7},{7,3},{8,12},{12,8},{9,1... | collective-permute-start | bytes 1376264 | tf_op jit(solution)/shard_map/ppermute | solution.py:34
  58.5 1.3 collective-permute-start.7
  59.8 1.5 collective-permute-start.8
  61.2 0.9 add.20
  62.1 11.0 %all-to-all-start = ((f32[32,7,4,128]{3,2,1,0:T(4,128)}), f32[32,7,4,128]{3,2,1,0:T(4,128)S(1)}, u32[]{:S(2)}, u32[]{:S(2)}) async-start(f32[32,7,4,128]{3,2,1,0:T(4,128)} %bitcast.3), calls=%async_computation | async-start | bytes 917504 | tf_op jit(solution)/shard_map/all_to_all | solution.py:398
  73.2 11.1 %collective-permute-done.7.refs_0_ = bf16[1984,256]{1,0:T(8,128)(2,1)} collective-permute-done((bf16[1984,256]{1,0:T(8,128)(2,1)}, bf16[1984,256]{1,0:T(8,128)(2,1)}, u32[]{:S(2)}, u32[]{:S(2)}) %collective-permute-start.7) | collective-permute-done | bytes 1015840 | tf_op jit(solution)/shard_map/ppermute | solution.py:34
  84.2 0.0 collective-permute-done.8.refs_2_
  84.3 4.0 %all-to-all-done.blocks_ref = f32[32,7,4,128]{3,2,1,0:T(4,128)S(1)} async-done(((f32[32,7,4,128]{3,2,1,0:T(4,128)}), f32[32,7,4,128]{3,2,1,0:T(4,128)S(1)}, u32[]{:S(2)}, u32[]{:S(2)}) %all-to-all-start) | async-done | bytes 458784 | tf_op jit(solution)/shard_map/all_to_all | solution.py:398
  88.3 0.9 summed_copies.1
  89.2 7.0 %all-to-all-start.1 = ((f32[32,7,4,128]{3,2,1,0:T(4,128)}), f32[32,7,4,128]{3,2,1,0:T(4,128)S(1)}, u32[]{:S(2)}, u32[]{:S(2)}) async-start(f32[32,7,4,128]{3,2,1,0:T(4,128)} %summed_copies.1), calls=%async_computation.1 | async-start | bytes 917504 | tf_op jit(solution)/shard_map/all_to_all | solution.py:402
  96.2 2.3 %collective-permute-start.11 = (bf16[1984,256]{1,0:T(8,128)(2,1)}, bf16[1984,256]{1,0:T(8,128)(2,1)}, u32[]{:S(2)}, u32[]{:S(2)}) collective-permute-start(bf16[1984,256]{1,0:T(8,128)(2,1)} %get-tuple-element.44), channel_id=1, source_target_pairs={{0,2},{1,3},{2,0},{3,1},{4,6},{5,7},{6,4},{7,5},{8,10},{9,11},{10,... | collective-permute-start | bytes 3047432 | tf_op jit(solution)/shard_map/ppermute | solution.py:34
  98.5 12.1 %all-to-all-done.1 = f32[32,7,4,128]{3,2,1,0:T(4,128)S(1)} async-done(((f32[32,7,4,128]{3,2,1,0:T(4,128)}), f32[32,7,4,128]{3,2,1,0:T(4,128)S(1)}, u32[]{:S(2)}, u32[]{:S(2)}) %all-to-all-start.1) | async-done | bytes 458784 | tf_op jit(solution)/shard_map/all_to_all | solution.py:402
  110.6 3.1 %collective-permute-start.9 = (f32[8,4,7,4,128]{4,3,2,1,0:T(4,128)S(1)}, f32[8,4,7,4,128]{4,3,2,1,0:T(4,128)S(1)}, u32[]{:S(2)}, u32[]{:S(2)}) collective-permute-start(f32[8,4,7,4,128]{4,3,2,1,0:T(4,128)S(1)} %bitcast.7), channel_id=1, source_target_pairs={{0,4},{4,0},{1,5},{5,1},{2,6},{6,2},{3,7},{7,3},{8,12},{12,8},{9,1... | collective-permute-start | bytes 1376264 | tf_op jit(solution)/shard_map/ppermute | solution.py:34
  113.7 1.4 collective-permute-done.9.other_ref
  115.2 2.0 %copy-done.1 = f32[3584,256]{1,0:T(8,128)S(1)} copy-done((f32[3584,256]{1,0:T(8,128)S(1)}, f32[3584,256]{1,0:T(8,128)}, u32[]{:S(2)}) %copy-start.1) | copy-done | bytes 3670040
  117.2 2.6 %cross_and_gram.1 = (f32[64,3584]{1,0:T(8,128)S(1)}, f32[64,256]{1,0:T(8,128)S(1)}, f32[64,64]{1,0:T(8,128)S(1)}) custom-call(s32[1]{0:T(128)} %bitcast.core_ref, f32[8,4,7,4,128]{4,3,2,1,0:T(4,128)S(1)} %bitcast.8, f32[8,4,7,4,128]{4,3,2,1,0:T(4,128)S(1)} %collective-permute-done.9.other_ref, f32[3584,256]{1,0:T(8,128)S(1)} %copy-done.1), custom_call_target="tpu_custom_call" | custom-call | flops 1000 | bytes 1000 | tf_op jit(solution)/shard_map/cross_and_gram/pallas_call | solution.py:144
  119.8 0.0 copy-start.7
  119.8 0.9 copy-done.7
  120.7 0.4 collective-permute-start.10
  121.1 0.9 collective-permute-done.10
  121.9 0.7 broadcast_in_dim.6
  122.6 3.3 %all-to-all-start.2 = ((f32[4,32,256]{2,1,0:T(8,128)}), f32[4,32,256]{2,1,0:T(8,128)S(1)}, u32[]{:S(2)}, u32[]{:S(2)}) async-start(f32[4,32,256]{2,1,0:T(8,128)} %broadcast_in_dim.6), calls=%async_computation.2 | async-start | bytes 262144 | tf_op jit(solution)/shard_map/all_to_all | solution.py:412
  125.9 3.0 %inverse_factor.1.inverse_ref = f32[64,64]{1,0:T(8,128)} custom-call(f32[64,64]{1,0:T(8,128)} %copy-done.11), custom_call_target="tpu_custom_call" | custom-call | flops 1000 | bytes 1000 | tf_op jit(solution)/shard_map/inverse_factor/pallas_call | solution.py:207
  129.0 1.8 %all-to-all-done.2 = f32[4,32,256]{2,1,0:T(8,128)S(1)} async-done(((f32[4,32,256]{2,1,0:T(8,128)}), f32[4,32,256]{2,1,0:T(8,128)S(1)}, u32[]{:S(2)}, u32[]{:S(2)}) %all-to-all-start.2) | async-done | bytes 131104 | tf_op jit(solution)/shard_map/all_to_all | solution.py:412
  130.7 0.0 collective-permute-done.11.refs_1_
  130.8 1.7 %collective-permute-start.12 = (bf16[1984,256]{1,0:T(8,128)(2,1)}, bf16[1984,256]{1,0:T(8,128)(2,1)}, u32[]{:S(2)}, u32[]{:S(2)}) collective-permute-start(bf16[1984,256]{1,0:T(8,128)(2,1)} %collective-permute-done.7.refs_0_), channel_id=1, source_target_pairs={{0,4},{4,0},{1,5},{5,1},{2,6},{6,2},{3,7},{7,3},{8,12},{12,8},{9,1... | collective-permute-start | bytes 3047432 | tf_op jit(solution)/shard_map/ppermute | solution.py:34
  132.5 0.1 collective-permute-start.13
  132.6 0.4 collective-permute-start.14
  133.0 0.7 broadcast_in_dim.7
  133.7 3.4 %all-to-all-start.3 = ((f32[8,32,256]{2,1,0:T(8,128)}), f32[8,32,256]{2,1,0:T(8,128)S(1)}, u32[]{:S(2)}, u32[]{:S(2)}) async-start(f32[8,32,256]{2,1,0:T(8,128)} %broadcast_in_dim.7), calls=%async_computation.3 | async-start | bytes 524288 | tf_op jit(solution)/shard_map/all_to_all | solution.py:420
  137.1 0.0 copy-start.8
  137.1 1.2 copy-done.8
  138.3 0.8 copy-done.9
  139.1 2.4 %orthonormal.1.basis_ref = bf16[3584,128]{1,0:T(8,128)(2,1)S(1)} custom-call(f32[64,64]{1,0:T(8,128)S(1)} %copy-done.9, f32[64,3584]{1,0:T(8,128)S(1)} %copy-done.8), custom_call_target="tpu_custom_call" | custom-call | flops 1000 | bytes 1000 | tf_op jit(solution)/shard_map/orthonormal/pallas_call | solution.py:222
  141.5 0.0 collective-permute-done.14.refs_5_
  141.5 6.2 %input_gradient.1 = bf16[192,3584]{1,0:T(8,128)(2,1)} custom-call(s32[1]{0:T(128)} %bitcast.core_ref, bf16[192,256]{1,0:T(8,128)(2,1)S(1)} %get-tuple-element.60.grad_ref, bf16[3584,256]{1,0:T(8,128)(2,1)S(1)} %copy-done.5, bf16[1984,256]{1,0:T(8,128)(2,1)} %collective-permute-done.7.refs_0_, bf16[1984,256]{1,0:T(8,128)(2,1)} %collective-permute-done.11.refs_1_, ...), custom_call_target="tpu_custom_call" | custom-call | flops 1000 | bytes 1000 | tf_op jit(solution)/shard_map/input_gradient/pallas_call | solution.py:299
  147.7 1.7 %all-to-all-done.3 = f32[8,32,256]{2,1,0:T(8,128)S(1)} async-done(((f32[8,32,256]{2,1,0:T(8,128)}), f32[8,32,256]{2,1,0:T(8,128)S(1)}, u32[]{:S(2)}, u32[]{:S(2)}) %all-to-all-start.3) | async-done | bytes 262176 | tf_op jit(solution)/shard_map/all_to_all | solution.py:420
  149.5 0.5 collective-permute-start.15
  150.0 0.9 collective-permute-done.15.other_ref
  150.8 2.0 %copy-done.2 = f32[3584,256]{1,0:T(8,128)S(1)} copy-done((f32[3584,256]{1,0:T(8,128)S(1)}, f32[3584,256]{1,0:T(8,128)}, u32[]{:S(2)}) %copy-start.2) | copy-done | bytes 3670040
  152.9 2.6 %finish.1 = (bf16[3584,256]{1,0:T(8,128)(2,1)}, f32[64,256]{1,0:T(8,128)}) custom-call(s32[1]{0:T(128)} %bitcast.core_ref, f32[32,256]{1,0:T(8,128)S(1)} %reduce_sum.19.mine_ref, f32[32,256]{1,0:T(8,128)S(1)} %collective-permute-done.15.other_ref, f32[64,64]{1,0:T(8,128)S(1)} %copy-done.9, bf16[3584,128]{1,0:T(8,128)(2,1)S(1)} %orthonormal.1.basis_ref, ...), custom_call_target="tpu_custom_call" | custom-call | flops 1000 | bytes 1000 | tf_op jit(solution)/shard_map/finish/pallas_call | solution.py:252
  (20 shorter events, 0.1 us)
Async XLA Ops:
  0.6 1.3 copy-start.3
  2.0 21.3 %copy-start.5 = (bf16[3584,256]{1,0:T(8,128)(2,1)S(1)}, bf16[3584,256]{1,0:T(8,128)(2,1)}, u32[]{:S(2)}) copy-start(bf16[3584,256]{1,0:T(8,128)(2,1)} %weight_ref.1) | copy-start | bytes 5505028
  3.1 17.0 %collective-permute-start = (bf16[96,3584]{1,0:T(8,128)(2,1)}, bf16[96,3584]{1,0:T(8,128)(2,1)S(1)}, u32[]{:S(2)}, u32[]{:S(2)}) collective-permute-start(bf16[96,3584]{1,0:T(8,128)(2,1)} %get-tuple-element.30), channel_id=1, source_target_pairs={{0,1},{1,2},{2,3},{3,0},{4,5},{5,6},{6,7},{7,4},{8,9},{9,10},{10,1... | collective-permute-start | bytes 2064392 | tf_op jit(solution)/shard_map/ppermute | solution.py:34
  5.3 16.3 %collective-permute-start.2 = (bf16[96,3584]{1,0:T(8,128)(2,1)}, bf16[96,3584]{1,0:T(8,128)(2,1)S(1)}, u32[]{:S(2)}, u32[]{:S(2)}) collective-permute-start(bf16[96,3584]{1,0:T(8,128)(2,1)} %get-tuple-element.31), channel_id=1, source_target_pairs={{0,3},{1,0},{2,1},{3,2},{4,7},{5,4},{6,5},{7,6},{8,11},{9,8},{10,9... | collective-permute-start | bytes 2064392 | tf_op jit(solution)/shard_map/ppermute | solution.py:34
  6.8 28.1 %collective-permute-start.5 = (bf16[96,3584]{1,0:T(8,128)(2,1)}, bf16[96,3584]{1,0:T(8,128)(2,1)}, u32[]{:S(2)}, u32[]{:S(2)}) collective-permute-start(bf16[96,3584]{1,0:T(8,128)(2,1)} %get-tuple-element.31), channel_id=1, source_target_pairs={{0,1},{1,2},{2,3},{3,0},{4,5},{5,6},{6,7},{7,4},{8,9},{9,10},{10,1... | collective-permute-start | bytes 2064392 | tf_op jit(solution)/shard_map/ppermute | solution.py:34
  6.8 29.3 %collective-permute-start.4 = (bf16[96,3584]{1,0:T(8,128)(2,1)}, bf16[96,3584]{1,0:T(8,128)(2,1)}, u32[]{:S(2)}, u32[]{:S(2)}) collective-permute-start(bf16[96,3584]{1,0:T(8,128)(2,1)} %get-tuple-element.30), channel_id=1, source_target_pairs={{0,3},{1,0},{2,1},{3,2},{4,7},{5,4},{6,5},{7,6},{8,11},{9,8},{10,9... | collective-permute-start | bytes 2064392 | tf_op jit(solution)/shard_map/ppermute | solution.py:34
  20.1 29.5 %collective-permute-start.1 = (bf16[96,3584]{1,0:T(8,128)(2,1)S(1)}, bf16[96,3584]{1,0:T(8,128)(2,1)S(1)}, u32[]{:S(2)}, u32[]{:S(2)}) collective-permute-start(bf16[96,3584]{1,0:T(8,128)(2,1)S(1)} %collective-permute-done.refs_3_), channel_id=1, source_target_pairs={{0,1},{1,2},{2,3},{3,0},{4,5},{5,6},{6,7},{7,4},{8,9},{9,10},{10,1... | collective-permute-start | bytes 2064392 | tf_op jit(solution)/shard_map/ppermute | solution.py:34
  21.6 29.1 %collective-permute-start.3 = (bf16[96,3584]{1,0:T(8,128)(2,1)S(1)}, bf16[96,3584]{1,0:T(8,128)(2,1)S(1)}, u32[]{:S(2)}, u32[]{:S(2)}) collective-permute-start(bf16[96,3584]{1,0:T(8,128)(2,1)S(1)} %collective-permute-done.2.refs_2_), channel_id=1, source_target_pairs={{0,3},{1,0},{2,1},{3,2},{4,7},{5,4},{6,5},{7,6},{8,11},{9,8},{10,9... | collective-permute-start | bytes 2064392 | tf_op jit(solution)/shard_map/ppermute | solution.py:34
  23.4 12.7 %copy-start.4 = (bf16[192,3584]{1,0:T(8,128)(2,1)S(1)}, bf16[192,3584]{1,0:T(8,128)(2,1)}, u32[]{:S(2)}) copy-start(bf16[192,3584]{1,0:T(8,128)(2,1)} %refs_0_.1) | copy-start | bytes 4128772
  23.4 12.7 %copy-start.6 = (bf16[1,3584,256]{2,1,0:T(8,128)(2,1)S(1)}, bf16[1,3584,256]{2,1,0:T(8,128)(2,1)}, u32[]{:S(2)}) copy-start(bf16[1,3584,256]{2,1,0:T(8,128)(2,1)} %param.8) | copy-start | bytes 5505028
  36.1 14.6 %copy-start.10 = (f32[256,64]{0,1:T(8,128)S(1)}, f32[256,64]{0,1:T(8,128)}, u32[]{:S(2)}) copy-start(f32[256,64]{0,1:T(8,128)} %param.9) | copy-start | bytes 196612
  54.6 1.8 %copy-start = (f32[3584,256]{1,0:T(8,128)}, f32[3584,256]{1,0:T(8,128)S(1)}, u32[]{:S(2)}) copy-start(f32[3584,256]{1,0:T(8,128)S(1)} %get-tuple-element.40.merged_ref) | copy-start | bytes 11010052
  56.4 4.9 %collective-permute-start.6 = (f32[8,4,7,4,128]{4,3,2,1,0:T(4,128)S(1)}, f32[8,4,7,4,128]{4,3,2,1,0:T(4,128)S(1)}, u32[]{:S(2)}, u32[]{:S(2)}) collective-permute-start(f32[8,4,7,4,128]{4,3,2,1,0:T(4,128)S(1)} %get-tuple-element.34), channel_id=1, source_target_pairs={{0,4},{4,0},{1,5},{5,1},{2,6},{6,2},{3,7},{7,3},{8,12},{12,8},{9,1... | collective-permute-start | bytes 1376264 | tf_op jit(solution)/shard_map/ppermute | solution.py:34
  58.5 25.8 %collective-permute-start.7 = (bf16[1984,256]{1,0:T(8,128)(2,1)}, bf16[1984,256]{1,0:T(8,128)(2,1)}, u32[]{:S(2)}, u32[]{:S(2)}) collective-permute-start(bf16[1984,256]{1,0:T(8,128)(2,1)} %get-tuple-element.37), channel_id=1, source_target_pairs={{0,1},{1,2},{2,3},{3,0},{4,5},{5,6},{6,7},{7,4},{8,9},{9,10},{10,1... | collective-permute-start | bytes 3047432 | tf_op jit(solution)/shard_map/ppermute | solution.py:34
  59.8 24.5 %collective-permute-start.8 = (bf16[1984,256]{1,0:T(8,128)(2,1)}, bf16[1984,256]{1,0:T(8,128)(2,1)}, u32[]{:S(2)}, u32[]{:S(2)}) collective-permute-start(bf16[1984,256]{1,0:T(8,128)(2,1)} %get-tuple-element.38), channel_id=1, source_target_pairs={{0,3},{1,0},{2,1},{3,2},{4,7},{5,4},{6,5},{7,6},{8,11},{9,8},{10,9... | collective-permute-start | bytes 3047432 | tf_op jit(solution)/shard_map/ppermute | solution.py:34
  62.1 26.1 %all-to-all-start = ((f32[32,7,4,128]{3,2,1,0:T(4,128)}), f32[32,7,4,128]{3,2,1,0:T(4,128)S(1)}, u32[]{:S(2)}, u32[]{:S(2)}) async-start(f32[32,7,4,128]{3,2,1,0:T(4,128)} %bitcast.3), calls=%async_computation | async-start | bytes 917504 | tf_op jit(solution)/shard_map/all_to_all | solution.py:398
  89.2 21.4 %all-to-all-start.1 = ((f32[32,7,4,128]{3,2,1,0:T(4,128)}), f32[32,7,4,128]{3,2,1,0:T(4,128)S(1)}, u32[]{:S(2)}, u32[]{:S(2)}) async-start(f32[32,7,4,128]{3,2,1,0:T(4,128)} %summed_copies.1), calls=%async_computation.1 | async-start | bytes 917504 | tf_op jit(solution)/shard_map/all_to_all | solution.py:402
  96.2 34.6 %collective-permute-start.11 = (bf16[1984,256]{1,0:T(8,128)(2,1)}, bf16[1984,256]{1,0:T(8,128)(2,1)}, u32[]{:S(2)}, u32[]{:S(2)}) collective-permute-start(bf16[1984,256]{1,0:T(8,128)(2,1)} %get-tuple-element.44), channel_id=1, source_target_pairs={{0,2},{1,3},{2,0},{3,1},{4,6},{5,7},{6,4},{7,5},{8,10},{9,11},{10,... | collective-permute-start | bytes 3047432 | tf_op jit(solution)/shard_map/ppermute | solution.py:34
  110.6 4.6 %collective-permute-start.9 = (f32[8,4,7,4,128]{4,3,2,1,0:T(4,128)S(1)}, f32[8,4,7,4,128]{4,3,2,1,0:T(4,128)S(1)}, u32[]{:S(2)}, u32[]{:S(2)}) collective-permute-start(f32[8,4,7,4,128]{4,3,2,1,0:T(4,128)S(1)} %bitcast.7), channel_id=1, source_target_pairs={{0,4},{4,0},{1,5},{5,1},{2,6},{6,2},{3,7},{7,3},{8,12},{12,8},{9,1... | collective-permute-start | bytes 1376264 | tf_op jit(solution)/shard_map/ppermute | solution.py:34
  115.2 2.0 %copy-start.1 = (f32[3584,256]{1,0:T(8,128)S(1)}, f32[3584,256]{1,0:T(8,128)}, u32[]{:S(2)}) copy-start(f32[3584,256]{1,0:T(8,128)} %copy-done) | copy-start | bytes 11010052
  119.8 0.9 copy-start.7
  120.7 5.2 %copy-start.11 = (f32[64,64]{1,0:T(8,128)}, f32[64,64]{1,0:T(8,128)S(1)}, u32[]{:S(2)}) copy-start(f32[64,64]{1,0:T(8,128)S(1)} %get-tuple-element.42.gram_ref) | copy-start | bytes 49156
  120.7 1.2 collective-permute-start.10
  122.6 8.1 %all-to-all-start.2 = ((f32[4,32,256]{2,1,0:T(8,128)}), f32[4,32,256]{2,1,0:T(8,128)S(1)}, u32[]{:S(2)}, u32[]{:S(2)}) async-start(f32[4,32,256]{2,1,0:T(8,128)} %broadcast_in_dim.6), calls=%async_computation.2 | async-start | bytes 262144 | tf_op jit(solution)/shard_map/all_to_all | solution.py:412
  130.8 10.7 %collective-permute-start.12 = (bf16[1984,256]{1,0:T(8,128)(2,1)}, bf16[1984,256]{1,0:T(8,128)(2,1)}, u32[]{:S(2)}, u32[]{:S(2)}) collective-permute-start(bf16[1984,256]{1,0:T(8,128)(2,1)} %collective-permute-done.7.refs_0_), channel_id=1, source_target_pairs={{0,4},{4,0},{1,5},{5,1},{2,6},{6,2},{3,7},{7,3},{8,12},{12,8},{9,1... | collective-permute-start | bytes 3047432 | tf_op jit(solution)/shard_map/ppermute | solution.py:34
  132.5 9.0 %collective-permute-start.13 = (bf16[1984,256]{1,0:T(8,128)(2,1)}, bf16[1984,256]{1,0:T(8,128)(2,1)}, u32[]{:S(2)}, u32[]{:S(2)}) collective-permute-start(bf16[1984,256]{1,0:T(8,128)(2,1)} %collective-permute-done.11.refs_1_), channel_id=1, source_target_pairs={{0,4},{4,0},{1,5},{5,1},{2,6},{6,2},{3,7},{7,3},{8,12},{12,8},{9,1... | collective-permute-start | bytes 3047432 | tf_op jit(solution)/shard_map/ppermute | solution.py:34
  132.6 8.9 %collective-permute-start.14 = (bf16[1984,256]{1,0:T(8,128)(2,1)}, bf16[1984,256]{1,0:T(8,128)(2,1)}, u32[]{:S(2)}, u32[]{:S(2)}) collective-permute-start(bf16[1984,256]{1,0:T(8,128)(2,1)} %collective-permute-done.8.refs_2_), channel_id=1, source_target_pairs={{0,4},{4,0},{1,5},{5,1},{2,6},{6,2},{3,7},{7,3},{8,12},{12,8},{9,1... | collective-permute-start | bytes 3047432 | tf_op jit(solution)/shard_map/ppermute | solution.py:34
  133.7 15.7 %all-to-all-start.3 = ((f32[8,32,256]{2,1,0:T(8,128)}), f32[8,32,256]{2,1,0:T(8,128)S(1)}, u32[]{:S(2)}, u32[]{:S(2)}) async-start(f32[8,32,256]{2,1,0:T(8,128)} %broadcast_in_dim.7), calls=%async_computation.3 | async-start | bytes 524288 | tf_op jit(solution)/shard_map/all_to_all | solution.py:420
  137.1 1.2 copy-start.8
  138.3 0.8 copy-start.9
  149.5 1.4 collective-permute-start.15
  150.8 2.0 %copy-start.2 = (f32[3584,256]{1,0:T(8,128)S(1)}, f32[3584,256]{1,0:T(8,128)}, u32[]{:S(2)}) copy-start(f32[3584,256]{1,0:T(8,128)} %copy-done) | copy-start | bytes 11010052
